TPU v7x, 128 devices: a whole 4x4x4 slice. The times are simulated.
128 devices in a mesh: dp: 8 (over x, z_lo), seq: 16 (over y, z_hi, core).
Axes of the slice: x: 4, y: 4, z: 4 (z_hi: 2, z_lo: 2; z = z_hi * 2 + z_lo), core: 2. Of those that a mesh axis runs over, the one named last changes fastest.
Arguments:
- tokens: bfloat16 [8, 2048, 2048], P('dp', 'seq'), may hold values from -6 to 6
- cotangent: bfloat16 [8, 2048, 2048], P('dp', 'seq'), may hold values from -6 to 6
- w_qkv: float32 [2048, 2560], P(('dp', 'seq')), may hold values from -0.21875 to 0.21875
- w_out: float32 [2048, 2048], P(('dp', 'seq')), may hold values from -0.125 to 0.125
- w_gate_up: float32 [2048, 11264], P(('dp', 'seq')), may hold values from -0.125 to 0.125
- w_down_t: float32 [2048, 5632], P(('dp', 'seq')), may hold values from -0.078125 to 0.078125
- gains: float32 [2048, 2], P(('dp', 'seq')), may hold values from 0.5 to 1.5
- first_qkv: float32 [2048, 2560], P(('dp', 'seq')), may hold values from -224 to 224
- second_qkv: float32 [2048, 2560], P(('dp', 'seq')), may hold values from 819.2 to 16384
- first_out: float32 [2048, 2048], P(('dp', 'seq')), may hold values from -112 to 112
- second_out: float32 [2048, 2048], P(('dp', 'seq')), may hold values from 819.2 to 6553.6
- first_gate_up: float32 [2048, 11264], P(('dp', 'seq')), may hold values from -56 to 56
- second_gate_up: float32 [2048, 11264], P(('dp', 'seq')), may hold values from 163.84 to 1310.72
- first_down: float32 [2048, 5632], P(('dp', 'seq')), may hold values from -56 to 56
- second_down: float32 [2048, 5632], P(('dp', 'seq')), may hold values from 163.84 to 1310.72
- first_gains: float32 [2048, 2], P(('dp', 'seq')), may hold values from -112 to 112
- second_gains: float32 [2048, 2], P(('dp', 'seq')), may hold values from 819.2 to 6553.6
Outputs:
- block_out: bfloat16 [8, 2048, 2048], P('dp', 'seq')
- d_tokens: bfloat16 [8, 2048, 2048], P('dp', 'seq')
- new_first_qkv: float32 [2048, 2560], P(('dp', 'seq'))
- new_second_qkv: float32 [2048, 2560], P(('dp', 'seq'))
- new_w_qkv: float32 [2048, 2560], P(('dp', 'seq'))
- new_first_out: float32 [2048, 2048], P(('dp', 'seq'))
- new_second_out: float32 [2048, 2048], P(('dp', 'seq'))
- new_w_out: float32 [2048, 2048], P(('dp', 'seq'))
- new_first_gate_up: float32 [2048, 11264], P(('dp', 'seq'))
- new_second_gate_up: float32 [2048, 11264], P(('dp', 'seq'))
- new_w_gate_up: float32 [2048, 11264], P(('dp', 'seq'))
- new_first_down: float32 [2048, 5632], P(('dp', 'seq'))
- new_second_down: float32 [2048, 5632], P(('dp', 'seq'))
- new_w_down: float32 [2048, 5632], P(('dp', 'seq'))
- new_first_gains: float32 [2048, 2], P(('dp', 'seq'))
- new_second_gains: float32 [2048, 2], P(('dp', 'seq'))
- new_gains: float32 [2048, 2], P(('dp', 'seq'))
All inputs are finite; a program needn't handle non-finite values.
Results may differ from a plain program's by a relative error of at most 0.034.
Values may be sent and summed in bfloat16 or wider, within the bound.
A program may use at most 320 MiB of HBM per device.

v0:
```python
import math

import jax
import jax.numpy as jnp
from jax import lax
from jax.sharding import PartitionSpec as P

D = 2048
KV_HEADS = 4
HEAD = 64
FF = 5632
STEP = 10


norm_eps = 1e-05
rope_base = 10000.0
mask_fill = -1e30
beta_one = 0.9
beta_two = 0.95
adam_eps = 1e-08
decay_rate = 0.1
rate_matrix = 0.08
rate_gain = 0.8


def rope_tables(length):
    half_width = HEAD // 2
    frequency = jnp.exp(
        jnp.arange(half_width, dtype=jnp.float32) * (-2.0 * math.log(rope_base) / HEAD)
    )
    angles = jnp.arange(length, dtype=jnp.float32)[:, None] * frequency[None, :]
    angles = jnp.concatenate([angles, angles], axis=1)
    return (jnp.cos(angles), jnp.sin(angles))


def rotate(values, cos_table, sin_table):
    half_width = values.shape[-1] // 2
    turned = jnp.concatenate([-values[..., half_width:], values[..., :half_width]], axis=-1)
    return values * cos_table + turned * sin_table


def rotate_back(grad_in, cos_table, sin_table):
    half_width = grad_in.shape[-1] // 2
    scaled = grad_in * sin_table
    turned = jnp.concatenate([scaled[..., half_width:], -scaled[..., :half_width]], axis=-1)
    return grad_in * cos_table + turned


def norm_stats(values):
    inverse = lax.rsqrt(jnp.mean(values * values, axis=-1, keepdims=True) + norm_eps)
    return (values * inverse, inverse)


def norm_back(grad_in, normed, inverse, gain_col):
    scaled = grad_in * gain_col
    input_grad = inverse * (scaled - normed * jnp.mean(scaled * normed, axis=-1, keepdims=True))
    return (input_grad, jnp.sum(grad_in * normed, axis=0))


def contract_last(left_side, right_side):
    return lax.dot_general(
        left_side, right_side, (((1,), (1,)), ((), ())), preferred_element_type=jnp.float32
    )


def contract_first(left_side, right_side):
    return lax.dot_general(
        left_side, right_side, (((0,), (0,)), ((), ())), preferred_element_type=jnp.float32
    )


def masked_scores(query_block, keys_rot, offset):
    block_rows = query_block.shape[0]
    length = keys_rot.shape[0]
    scores = jnp.einsum(
        "bhe,le->hbl", query_block, keys_rot, preferred_element_type=jnp.float32
    ) * HEAD ** (-0.5)
    query_pos = offset + jnp.arange(block_rows, dtype=jnp.int32)
    key_pos = jnp.arange(length, dtype=jnp.int32)
    return jnp.where(key_pos[None, None, :] <= query_pos[None, :, None], scores, mask_fill)


def head_attention(query_heads, kv_heads):
    length = query_heads.shape[0]
    heads_here = query_heads.shape[1] // HEAD
    cos_table, sin_table = rope_tables(length)
    queries = rotate(
        query_heads.astype(jnp.float32).reshape(length, heads_here, HEAD),
        cos_table[:, None, :],
        sin_table[:, None, :],
    ).astype(jnp.bfloat16)
    keys_rot = rotate(kv_heads[:, :HEAD].astype(jnp.float32), cos_table, sin_table).astype(
        jnp.bfloat16
    )
    values = kv_heads[:, HEAD:]
    block_rows = min(512, length)

    def one_block(offset):
        query_block = lax.dynamic_slice_in_dim(queries, offset, block_rows, 0)
        scores = masked_scores(query_block, keys_rot, offset)
        totals = jax.nn.logsumexp(scores, axis=-1, keepdims=True)
        attn_probs = jnp.exp(scores - totals).astype(jnp.bfloat16)
        mixed_rows = jnp.einsum(
            "hbl,le->bhe", attn_probs, values, preferred_element_type=jnp.float32
        )
        return (mixed_rows.astype(jnp.bfloat16), totals)

    offsets = jnp.arange(length // block_rows, dtype=jnp.int32) * block_rows
    mixed_rows, totals = lax.map(one_block, offsets)
    return (mixed_rows.reshape(length, heads_here * HEAD), totals, queries, keys_rot)


def head_attention_back(queries, keys_rot, values, totals, grad_heads):
    length = queries.shape[0]
    heads_here = queries.shape[1]
    block_rows = min(512, length)
    score_scale = HEAD ** (-0.5)
    grad_split = grad_heads.reshape(length, heads_here, HEAD)

    def one_step(carried, offset):
        key_grad, value_grad = carried
        query_block = lax.dynamic_slice_in_dim(queries, offset, block_rows, 0)
        grad_block = lax.dynamic_slice_in_dim(grad_split, offset, block_rows, 0)
        block_total = lax.dynamic_index_in_dim(totals, offset // block_rows, 0, keepdims=False)
        attn_probs = jnp.exp(masked_scores(query_block, keys_rot, offset) - block_total)
        prob_grad = jnp.einsum(
            "bhe,le->hbl", grad_block, values, preferred_element_type=jnp.float32
        )
        inner_sum = jnp.sum(attn_probs * prob_grad, axis=-1, keepdims=True)
        score_grad = (attn_probs * (prob_grad - inner_sum)).astype(jnp.bfloat16)
        query_grad = (
            jnp.einsum("hbl,le->bhe", score_grad, keys_rot, preferred_element_type=jnp.float32)
            * score_scale
        )
        key_grad = (
            key_grad
            + jnp.einsum("hbl,bhe->le", score_grad, query_block, preferred_element_type=jnp.float32)
            * score_scale
        )
        value_grad = value_grad + jnp.einsum(
            "hbl,bhe->le",
            attn_probs.astype(jnp.bfloat16),
            grad_block,
            preferred_element_type=jnp.float32,
        )
        return ((key_grad, value_grad), query_grad)

    zeros_kv = jnp.zeros((length, HEAD), jnp.float32)
    offsets = jnp.arange(length // block_rows, dtype=jnp.int32) * block_rows
    (key_grad, value_grad), query_grad = lax.scan(one_step, (zeros_kv, zeros_kv), offsets)
    cos_table, sin_table = rope_tables(length)
    query_grad = rotate_back(
        query_grad.reshape(length, heads_here, HEAD), cos_table[:, None, :], sin_table[:, None, :]
    )
    key_grad = rotate_back(key_grad, cos_table, sin_table)
    return (
        query_grad.reshape(length, heads_here * HEAD).astype(jnp.bfloat16),
        jnp.concatenate([key_grad, value_grad], axis=1),
    )


def owner_cols(matrix, dp_parts, seq_parts):
    tok_rows = matrix.shape[0]
    band = matrix.shape[1] // (dp_parts * seq_parts)
    arranged = (
        matrix.astype(jnp.float32)
        .reshape(tok_rows, dp_parts, seq_parts, band)
        .transpose(2, 0, 1, 3)
    )
    return arranged.reshape(seq_parts, tok_rows, dp_parts * band)


def owner_gains(vectors, dp_parts, seq_parts):
    columns = vectors.shape[1]
    band = vectors.shape[0] // (dp_parts * seq_parts)
    arranged = vectors.reshape(dp_parts, seq_parts, band, columns).transpose(1, 3, 0, 2)
    return arranged.reshape(seq_parts, columns, dp_parts * band)


def fold_rows(left_cols, pieces):
    return tuple((contract_first(left_side, piece) for left_side, piece in zip(left_cols, pieces)))


def adam(weight, gradient, first_moment, second, step_rate, decay_weight):
    first_new = beta_one * first_moment + (1.0 - beta_one) * gradient
    second_new = beta_two * second + (1.0 - beta_two) * gradient * gradient
    first_hat = first_new / (1.0 - beta_one**STEP)
    second_hat = second_new / (1.0 - beta_two**STEP)
    weight_new = weight - step_rate * (
        first_hat / (jnp.sqrt(second_hat) + adam_eps) + decay_weight * weight
    )
    return (first_new, second_new, weight_new)


def local(
    tokens,
    cotangent,
    w_qkv,
    w_out,
    w_gate_up,
    w_down_t,
    gains,
    first_qkv,
    second_qkv,
    first_out,
    second_out,
    first_gate_up,
    second_gate_up,
    first_down,
    second_down,
    first_gains,
    second_gains,
):
    inputs = tokens[0].astype(jnp.float32)
    back_rounded = cotangent[0]
    back_grad = back_rounded.astype(jnp.float32)
    tok_rows = inputs.shape[0]
    kv_width = KV_HEADS * HEAD
    qkv_width = D + 2 * kv_width
    seq_parts = lax.axis_size("seq")
    dp_parts = lax.axis_size("dp")
    copies_per = seq_parts // KV_HEADS
    low_shards = (
        w_qkv.astype(jnp.bfloat16),
        w_out.astype(jnp.bfloat16),
        w_gate_up.astype(jnp.bfloat16),
        w_down_t.astype(jnp.bfloat16),
        gains.astype(jnp.bfloat16),
    )
    gathered = (
        lax.all_gather(low_shards[0], ("dp", "seq"), axis=0, tiled=True),
        lax.all_gather(low_shards[1], ("dp", "seq"), axis=0, tiled=True),
        lax.all_gather(low_shards[2], ("dp", "seq"), axis=0, tiled=True),
        lax.all_gather(low_shards[3], ("dp", "seq"), axis=0, tiled=True),
        lax.all_gather(low_shards[4], ("dp", "seq"), axis=0, tiled=True),
    )
    qkv_full, out_full, gate_up_full, down_full, gain_full = gathered
    gain_wide = gain_full.astype(jnp.float32)
    normed_in, inverse_in = norm_stats(inputs)
    acts_in = (normed_in * gain_wide[:, 0]).astype(jnp.bfloat16)
    qkv_rows = jnp.dot(acts_in, qkv_full, preferred_element_type=jnp.float32).astype(jnp.bfloat16)
    key_part = qkv_rows[:, D : D + kv_width].reshape(tok_rows, KV_HEADS, HEAD)
    value_part = qkv_rows[:, D + kv_width :].reshape(tok_rows, KV_HEADS, HEAD)
    kv_copies = jnp.repeat(
        jnp.concatenate([key_part, value_part], axis=2), copies_per, axis=1
    ).reshape(tok_rows, seq_parts * 2 * HEAD)
    query_heads, kv_heads = (
        lax.all_to_all(qkv_rows[:, :D], "seq", split_axis=1, concat_axis=0, tiled=True),
        lax.all_to_all(kv_copies, "seq", split_axis=1, concat_axis=0, tiled=True),
    )
    mixed_heads, totals, queries, keys_rot = head_attention(query_heads, kv_heads)
    mixed_tok = lax.all_to_all(mixed_heads, "seq", split_axis=0, concat_axis=1, tiled=True)
    resid_mid = inputs + jnp.dot(mixed_tok, out_full, preferred_element_type=jnp.float32)
    normed_mid, inverse_mid = norm_stats(resid_mid)
    acts_mid = (normed_mid * gain_wide[:, 1]).astype(jnp.bfloat16)
    gate_up = jnp.dot(acts_mid, gate_up_full, preferred_element_type=jnp.float32)
    gate_rows = gate_up[:, :FF]
    up_rows = gate_up[:, FF:]
    silu_gate = jax.nn.silu(gate_rows)
    hidden = (silu_gate * up_rows).astype(jnp.bfloat16)
    block_out = (resid_mid + contract_last(hidden, down_full)).astype(jnp.bfloat16)
    qkv_back, out_back, gate_up_back, down_back, gain_back = (
        lax.all_gather(low_shards[0], ("dp", "seq"), axis=0, tiled=True),
        lax.all_gather(low_shards[1], ("dp", "seq"), axis=0, tiled=True),
        lax.all_gather(low_shards[2], ("dp", "seq"), axis=0, tiled=True),
        lax.all_gather(low_shards[3], ("dp", "seq"), axis=0, tiled=True),
        lax.all_gather(low_shards[4], ("dp", "seq"), axis=0, tiled=True),
    )
    gain_back_wide = gain_back.astype(jnp.float32)
    hidden_grad = jnp.dot(back_rounded, down_back, preferred_element_type=jnp.float32)
    sigmoid_gate = jax.nn.sigmoid(gate_rows)
    gate_grad = hidden_grad * up_rows * sigmoid_gate * (1.0 + gate_rows * (1.0 - sigmoid_gate))
    up_grad = hidden_grad * silu_gate
    gate_up_grad = jnp.concatenate([gate_grad, up_grad], axis=1).astype(jnp.bfloat16)
    acts_mid_grad = contract_last(gate_up_grad, gate_up_back)
    mid_norm_grad, gain_grad_mid = norm_back(
        acts_mid_grad, normed_mid, inverse_mid, gain_back_wide[:, 1]
    )
    mid_grad = back_grad + mid_norm_grad
    attn_grad = mid_grad.astype(jnp.bfloat16)
    mixed_grad = contract_last(attn_grad, out_back).astype(jnp.bfloat16)
    grad_heads = lax.all_to_all(mixed_grad, "seq", split_axis=1, concat_axis=0, tiled=True)
    query_grad, kv_grad = head_attention_back(
        queries, keys_rot, kv_heads[:, HEAD:], totals, grad_heads
    )
    query_grad_tok = lax.all_to_all(query_grad, "seq", split_axis=0, concat_axis=1, tiled=True)
    kv_grad_tok = lax.all_to_all(
        kv_grad.astype(jnp.bfloat16), "seq", split_axis=0, concat_axis=1, tiled=True
    ).astype(kv_grad.dtype)
    kv_summed = jnp.sum(
        kv_grad_tok.reshape(tok_rows, KV_HEADS, copies_per, 2 * HEAD), axis=2
    ).astype(jnp.bfloat16)
    qkv_grad = jnp.concatenate(
        [
            query_grad_tok,
            kv_summed[:, :, :HEAD].reshape(tok_rows, kv_width),
            kv_summed[:, :, HEAD:].reshape(tok_rows, kv_width),
        ],
        axis=1,
    )
    acts_in_grad = contract_last(qkv_grad, qkv_back)
    in_norm_grad, gain_grad_in = norm_back(
        acts_in_grad, normed_in, inverse_in, gain_back_wide[:, 0]
    )
    d_tokens = (mid_grad + in_norm_grad).astype(jnp.bfloat16)
    gain_pair = jnp.stack([gain_grad_in, gain_grad_mid], axis=1)
    all_recv = (
        lax.all_to_all(
            owner_cols(acts_in, dp_parts, seq_parts).astype(jnp.bfloat16),
            "seq",
            split_axis=0,
            concat_axis=1,
            tiled=True,
        ).astype(jnp.float32),
        lax.all_to_all(
            owner_cols(mixed_tok, dp_parts, seq_parts).astype(jnp.bfloat16),
            "seq",
            split_axis=0,
            concat_axis=1,
            tiled=True,
        ).astype(jnp.float32),
        lax.all_to_all(
            owner_cols(acts_mid, dp_parts, seq_parts).astype(jnp.bfloat16),
            "seq",
            split_axis=0,
            concat_axis=1,
            tiled=True,
        ).astype(jnp.float32),
        lax.all_to_all(
            owner_cols(back_rounded, dp_parts, seq_parts).astype(jnp.bfloat16),
            "seq",
            split_axis=0,
            concat_axis=1,
            tiled=True,
        ).astype(jnp.float32),
        lax.all_to_all(
            owner_gains(gain_pair, dp_parts, seq_parts).astype(jnp.bfloat16),
            "seq",
            split_axis=0,
            concat_axis=1,
            tiled=True,
        ).astype(jnp.float32),
    )
    all_left = tuple((piece[0].astype(jnp.bfloat16) for piece in all_recv[:4]))
    all_gain = jnp.sum(all_recv[4][0].reshape(seq_parts, 2, -1), axis=0)
    all_rows = fold_rows(
        all_left,
        (
            lax.all_gather(qkv_grad, "seq", axis=0, tiled=True),
            lax.all_gather(attn_grad, "seq", axis=0, tiled=True),
            lax.all_gather(gate_up_grad, "seq", axis=0, tiled=True),
            lax.all_gather(hidden, "seq", axis=0, tiled=True),
        ),
    )
    all_term = jnp.concatenate(
        [all_rows[0], all_rows[1], all_rows[2], all_rows[3], all_gain.T], axis=1
    )
    summed = lax.psum_scatter(
        all_term.astype(jnp.bfloat16), "dp", scatter_dimension=0, tiled=True
    ).astype(jnp.float32)
    grad_qkv = summed[:, :qkv_width]
    grad_out = summed[:, qkv_width : qkv_width + D]
    grad_gate_up = summed[:, qkv_width + D : qkv_width + D + 2 * FF]
    grad_down = summed[:, qkv_width + D + 2 * FF : qkv_width + D + 3 * FF]
    grad_gains = summed[:, qkv_width + D + 3 * FF :]
    first_q, second_q, weight_q = adam(
        w_qkv, grad_qkv, first_qkv, second_qkv, rate_matrix, decay_rate
    )
    first_o, second_o, weight_o = adam(
        w_out, grad_out, first_out, second_out, rate_matrix, decay_rate
    )
    first_g, second_g, weight_g = adam(
        w_gate_up, grad_gate_up, first_gate_up, second_gate_up, rate_matrix, decay_rate
    )
    first_d, second_d, weight_d = adam(
        w_down_t, grad_down, first_down, second_down, rate_matrix, decay_rate
    )
    first_n, second_n, weight_n = adam(gains, grad_gains, first_gains, second_gains, rate_gain, 0.0)
    return (
        block_out[None],
        d_tokens[None],
        first_q,
        second_q,
        weight_q,
        first_o,
        second_o,
        weight_o,
        first_g,
        second_g,
        weight_g,
        first_d,
        second_d,
        weight_d,
        first_n,
        second_n,
        weight_n,
    )


def solution(mesh):
    return jax.shard_map(
        local,
        mesh=mesh,
        in_specs=(
            P("dp", "seq", None),
            P("dp", "seq", None),
            P(("dp", "seq"), None),
            P(("dp", "seq"), None),
            P(("dp", "seq"), None),
            P(("dp", "seq"), None),
            P(("dp", "seq"), None),
            P(("dp", "seq"), None),
            P(("dp", "seq"), None),
            P(("dp", "seq"), None),
            P(("dp", "seq"), None),
            P(("dp", "seq"), None),
            P(("dp", "seq"), None),
            P(("dp", "seq"), None),
            P(("dp", "seq"), None),
            P(("dp", "seq"), None),
            P(("dp", "seq"), None),
        ),
        out_specs=(
            P("dp", "seq", None),
            P("dp", "seq", None),
            P(("dp", "seq"), None),
            P(("dp", "seq"), None),
            P(("dp", "seq"), None),
            P(("dp", "seq"), None),
            P(("dp", "seq"), None),
            P(("dp", "seq"), None),
            P(("dp", "seq"), None),
            P(("dp", "seq"), None),
            P(("dp", "seq"), None),
            P(("dp", "seq"), None),
            P(("dp", "seq"), None),
            P(("dp", "seq"), None),
            P(("dp", "seq"), None),
            P(("dp", "seq"), None),
            P(("dp", "seq"), None),
        ),
        check_vma=False,
    )
```

profile of v0, /device:TPU:1, one launch (start us, length us, event | category | flops | bytes accessed | tf_op | source)
XLA Modules:
  0.0 1941.8 jit_solution(3779362817887169311)
XLA Ops:
  16.0 179.3 %all-gather = bf16[128,16,2]{1,2,0:T(2,128)(2,1)S(1)} all-gather(bf16[1,16,2]{1,2,0:T(2,128)(2,1)S(1)} %convert_bitcast_fusion.2), channel_id=1, replica_groups=mesh['dp'=8,'seq'=16] {'dp','seq'}, dimensions={0}, use_global_device_ids=true | all-gather | bytes 8256 | tf_op jit(solution)/shard_map/all_gather | solution.py:235
  197.5 22.4 %all-gather.10.cloned.1.call-done = bf16[2048,2560]{1,0:T(8,128)(2,1)} async-done(((bf16[16,2560]{1,0:T(8,128)(2,1)}), bf16[2048,2560]{1,0:T(8,128)(2,1)}) %all-gather.10.cloned.1.call-update) | async-done | bytes 10485776 | tf_op jit(solution)/shard_map/all_gather | solution.py:231
  219.9 5.6 convolution_convert_fusion.3
  226.6 6.0 all-to-all-start.1
  234.1 10.9 all-to-all-done.1
  245.0 5.1 all-to-all-start
  251.8 5.5 fusion.75
  269.0 48.9 %while.29 = (s32[]{:T(128)}, bf16[4,512,2,64]{1,3,2,0:T(8,128)(2,1)}, f32[4,2,512,1]{2,1,3,0:T(2,128)S(1)}, s32[4]{0:T(128)S(1)}, bf16[2048,2,64]{0,2,1:T(8,128)...) while((s32[]{:T(128)}, ...), condition=%wide.region_4.5_spmd, body=%wide.region_1.4_spmd.sunk | while | flops 561062400 | bytes 30200480 | solution.py:109
  320.5 5.9 all-to-all-start.2
  326.4 101.7 %all-gather.12.cloned.1.call-done = bf16[2048,2048]{1,0:T(8,128)(2,1)} async-done(((bf16[16,2048]{1,0:T(8,128)(2,1)}), bf16[2048,2048]{1,0:T(8,128)(2,1)}) %all-gather.12.cloned.1.call-update) | async-done | bytes 8388624 | tf_op jit(solution)/shard_map/all_gather | solution.py:232
  428.1 4.9 multiply_reduce_fusion.4
  433.3 256.0 %all-gather.14.cloned.1.call-done = bf16[2048,11264]{1,0:T(8,128)(2,1)} async-done(((bf16[16,11264]{1,0:T(8,128)(2,1)}), bf16[2048,11264]{1,0:T(8,128)(2,1)}) %all-gather.14.cloned.1.call-update) | async-done | bytes 46137360 | tf_op jit(solution)/shard_map/all_gather | solution.py:233
  689.3 20.1 %fusion.101 = f32[128,11264]{1,0:T(8,128)} fusion(bf16[128,2048]{1,0:T(8,128)(2,1)S(1)} %multiply_convert_fusion.4, bf16[2048,11264]{1,0:T(8,128)(2,1)} %all-gather.14.cloned.1.call-done), kind=kOutput, calls=%fused_computation.186 | convolution fusion | flops 5905580032 | bytes 52428800 | tf_op jit(solution)/shard_map/dot_general | solution.py:256
  709.4 206.1 %all-gather.16.cloned.1.call-done = bf16[2048,5632]{1,0:T(8,128)(2,1)} async-done(((bf16[16,5632]{1,0:T(8,128)(2,1)}), bf16[2048,5632]{1,0:T(8,128)(2,1)}) %all-gather.16.cloned.1.call-update) | async-done | bytes 23068688 | tf_op jit(solution)/shard_map/all_gather | solution.py:234
  915.5 15.5 multiply_convert_fusion.1
  931.0 22.1 %multiply_reduce_fusion = (bf16[2048]{0:T(1024)(128)(2,1)S(1)}, f32[128]{0:T(128)S(1)}, f32[128,2048]{1,0:T(8,128)S(1)}) fusion(f32[128,2048]{1,0:T(8,128)S(1)} %get-tuple-element.490, f32[128]{0:T(128)S(1)} %add_rsqrt_fusion, f32[2048]{0:T(1024)S(1)} %bitcast.322, bf16[2048,11264]{1,0:T(8,128)(2,1)} %all-gather.14.cloned.1.call-done, ...), kind=kOutput, calls=%fused_computation.120 | convolution fusion | flops 5912918016 | bytes 51131392 | tf_op jit(solution)/shard_map/dot_general | solution.py:61
  954.3 6.5 fusion.69
  961.8 6.2 all-to-all-start.3
  969.3 9.8 all-to-all-done.3
  979.8 130.4 %while.30 = (s32[]{:T(128)}, f32[2048,64]{0,1:T(8,128)S(1)}, f32[2048,64]{0,1:T(8,128)}, f32[4,512,2,64]{1,0,3,2:T(4,128)}, s32[4]{0:T(128)S(1)}, /*index=5*/bf1...) while((s32[]{:T(128)}, f32[2048,64]{0,1:T(8,128)S(1)}, ...), condition=%wide.region_9.10_spmd.clone, body=%wide.region_7.9_spmd.clone.sunk | while | flops 1375403520 | bytes 122192336 | solution.py:150
  997.2 6.1 dynamic_update_slice.23
  1006.6 5.6 fusion.162
  1029.7 6.1 dynamic_update_slice.23
  1039.0 5.8 fusion.162
  1062.3 6.1 dynamic_update_slice.23
  1071.6 5.8 fusion.162
  1094.9 6.1 dynamic_update_slice.23
  1104.2 5.8 fusion.162
  1122.7 4.7 fusion.76
  1130.9 4.7 all-to-all-start.5
  1139.6 7.2 all-to-all-done.5
  1146.8 4.7 all-to-all-start.4
  1151.7 11.0 all-to-all-done.4
  1169.9 4.7 all-to-all-start.6
  1177.6 11.8 all-to-all-done.6
  1189.4 4.1 all-to-all-start.9
  1194.4 9.9 all-to-all-done.9
  1204.2 4.7 all-to-all-start.7
  1211.9 8.2 all-to-all-done.7
  1220.2 5.0 all-to-all-start.8
  1225.3 9.1 multiply_reduce_fusion.1
  1236.5 5.9 all-to-all-start.10
  1249.5 16.8 all-gather.18.cloned.1.call-done
  1266.3 8.5 fusion.62
  1274.8 65.4 %all-gather.20.cloned.1.call-done = bf16[2048,2048]{1,0:T(8,128)(2,1)} async-done(((bf16[128,2048]{1,0:T(8,128)(2,1)}), bf16[2048,2048]{1,0:T(8,128)(2,1)}) %all-gather.20.cloned.1.call-update) | async-done | bytes 8388624 | tf_op jit(solution)/shard_map/all_gather | solution.py:350
  1340.2 5.5 fusion.66
  1345.7 240.4 %all-gather.22.cloned.1.call-done = bf16[2048,11264]{1,0:T(8,128)(2,1)} async-done(((bf16[128,11264]{1,0:T(8,128)(2,1)}), bf16[2048,11264]{1,0:T(8,128)(2,1)}) %all-gather.22.cloned.1.call-update) | async-done | bytes 46137360 | tf_op jit(solution)/shard_map/all_gather | solution.py:351
  1586.1 20.3 %fusion.58 = bf16[128,21506]{1,0:T(8,128)(2,1)} fusion(bf16[128,21506]{1,0:T(8,128)(2,1)} %fusion.66, bf16[2048,128]{1,0:T(8,128)(2,1)S(1)} %bitcast.301, bf16[2048,11264]{1,0:T(8,128)(2,1)} %all-gather.22.cloned.1.call-done), kind=kOutput, calls=%fused_computation.64 | convolution fusion | flops 5907021824 | bytes 49545216 | tf_op jit(solution)/shard_map/dot_general | solution.py:67
  1606.4 118.7 %all-gather.24.cloned.1.call-done = bf16[2048,5632]{1,0:T(8,128)(2,1)} async-done(((bf16[128,5632]{1,0:T(8,128)(2,1)}), bf16[2048,5632]{1,0:T(8,128)(2,1)}) %all-gather.24.cloned.1.call-update) | async-done | bytes 23068688 | tf_op jit(solution)/shard_map/all_gather | solution.py:352
  1725.1 12.0 fusion.60
  1738.4 4.1 copy.355
  1748.2 4.1 copy.354
  1757.6 4.1 copy.352
  1790.3 13.1 fusion.67
  1804.9 46.1 %reduce-scatter.4.cloned.1.call-done = bf16[16,21506]{1,0:T(8,128)(2,1)} async-done(((bf16[128,21506]{1,0:T(8,128)(2,1)}), bf16[16,21506]{1,0:T(8,128)(2,1)}) %reduce-scatter.4.cloned.1.call-update) | async-done | bytes 688208
  1851.0 5.3 copy.379
  1856.3 7.5 convert_element_type.235
  1863.8 15.3 multiply_subtract_fusion
  1879.1 5.0 copy.369
  1884.1 5.2 copy.370
  1889.2 5.0 copy.371
  1894.2 8.8 multiply_subtract_fusion.1
  1910.8 4.7 multiply_subtract_fusion.3
  1922.1 4.6 multiply_subtract_fusion.2
  (360 shorter events, 249.7 us)
Async XLA Ops:
  7.2 212.7 %copy-start.6 = (bf16[1,128,2048]{2,1,0:T(8,128)(2,1)S(1)}, bf16[1,128,2048]{2,1,0:T(8,128)(2,1)}, u32[]{:S(2)}) copy-start(bf16[1,128,2048]{2,1,0:T(8,128)(2,1)} %param.21) | copy-start | bytes 1572868
  7.2 212.7 %all-gather.10.cloned.1.call-start = ((), (), s32[]{:S(2)}) async-start(), calls=%async_computation.12 | async-start | bytes 10567680 | tf_op jit(solution)/shard_map/all_gather | solution.py:231
  9.0 419.1 %all-gather.12.cloned.1.call-start = ((), (), s32[]{:S(2)}) async-start(), calls=%async_computation.13 | async-start | bytes 8454144 | tf_op jit(solution)/shard_map/all_gather | solution.py:232
  10.8 678.5 %all-gather.14.cloned.1.call-start = ((), (), s32[]{:S(2)}) async-start(), calls=%async_computation.14 | async-start | bytes 46497792 | tf_op jit(solution)/shard_map/all_gather | solution.py:233
  13.3 902.2 %all-gather.16.cloned.1.call-start = ((), (), s32[]{:S(2)}) async-start(), calls=%async_computation.15 | async-start | bytes 23248896 | tf_op jit(solution)/shard_map/all_gather | solution.py:234
  196.8 28.6 %copy-start.53 = (f32[128]{0:T(128)}, f32[128]{0:T(128)S(1)}, u32[]{:S(2)}) copy-start(f32[128]{0:T(128)S(1)} %add_rsqrt_fusion.1) | copy-start | bytes 1540
  197.4 28.0 %copy-start.48 = (f32[2048,1]{0,1:T(1,128)}, f32[2048,1]{0,1:T(1,128)S(1)}, u32[]{:S(2)}) copy-start(f32[2048,1]{0,1:T(1,128)S(1)} %get-tuple-element.488) | copy-start | bytes 24580
  197.5 755.7 %copy-start.46 = (f32[2048,1]{0,1:T(1,128)}, f32[2048,1]{0,1:T(1,128)S(1)}, u32[]{:S(2)}) copy-start(f32[2048,1]{0,1:T(1,128)S(1)} %get-tuple-element.487) | copy-start | bytes 24580
  226.6 18.4 all-to-all-start.1
  232.9 24.4 %copy-start.4 = (f32[2048,32]{1,0:T(8,128)}, f32[2048,32]{1,0:T(8,128)S(1)}, u32[]{:S(2)}) copy-start(f32[2048,32]{1,0:T(8,128)S(1)} %iota_multiply_fusion) | copy-start | bytes 786436
  245.0 17.4 all-to-all-start
  257.3 9.1 copy-start.30
  258.9 10.1 copy-start.22
  260.6 8.3 copy-start.20
  320.5 107.7 %all-to-all-start.2 = ((bf16[16,128,128]{1,2,0:T(8,128)(2,1)}), bf16[16,128,128]{1,2,0:T(8,128)(2,1)S(1)}, u32[]{:S(2)}, u32[]{:S(2)}) async-start(bf16[16,128,128]{1,2,0:T(8,128)(2,1)} %copy.303), calls=%async_computation.2 | async-start | bytes 1048576 | tf_op jit(solution)/shard_map/all_to_all | solution.py:252
  433.1 520.1 %copy-start.2 = (f32[128,2048]{1,0:T(8,128)}, f32[128,2048]{1,0:T(8,128)S(1)}, u32[]{:S(2)}) copy-start(f32[128,2048]{1,0:T(8,128)S(1)} %get-tuple-element.490) | copy-start | bytes 3145732
  433.1 520.1 %copy-start.51 = (f32[128]{0:T(128)}, f32[128]{0:T(128)S(1)}, u32[]{:S(2)}) copy-start(f32[128]{0:T(128)S(1)} %add_rsqrt_fusion) | copy-start | bytes 1540
  433.3 276.1 %copy-start.18 = (bf16[128,2048]{1,0:T(8,128)(2,1)}, bf16[128,2048]{1,0:T(8,128)(2,1)S(1)}, u32[]{:S(2)}) copy-start(bf16[128,2048]{1,0:T(8,128)(2,1)S(1)} %multiply_convert_fusion.4) | copy-start | bytes 1572868
  433.3 482.3 %copy-start.24 = (bf16[1,128,2048]{2,1,0:T(8,128)(2,1)S(1)}, bf16[1,128,2048]{2,1,0:T(8,128)(2,1)}, u32[]{:S(2)}) copy-start(bf16[1,128,2048]{2,1,0:T(8,128)(2,1)} %param.22) | copy-start | bytes 1572868
  931.0 22.1 %copy-start.25 = (bf16[1,128,2048]{2,1,0:T(8,128)(2,1)S(1)}, bf16[1,128,2048]{2,1,0:T(8,128)(2,1)}, u32[]{:S(2)}) copy-start(bf16[1,128,2048]{2,1,0:T(8,128)(2,1)} %param.22) | copy-start | bytes 1572868
  954.3 13.7 copy-start.23
  961.8 17.3 all-to-all-start.3
  979.8 136.0 %copy-start.21 = (f32[2048,64]{0,1:T(8,128)S(1)}, f32[2048,64]{0,1:T(8,128)}, u32[]{:S(2)}) copy-start(f32[2048,64]{0,1:T(8,128)} %copy-done.20) | copy-start | bytes 1572868
  1110.1 8.4 copy-start.5
  1127.3 9.7 copy-start.27
  1130.9 15.9 all-to-all-start.5
  1136.9 27.4 %copy-start.15 = (bf16[128,5632]{1,0:T(8,128)(2,1)S(1)}, bf16[128,5632]{1,0:T(8,128)(2,1)}, u32[]{:S(2)}) copy-start(bf16[128,5632]{1,0:T(8,128)(2,1)} %get-tuple-element.458) | copy-start | bytes 4325380
  1146.8 15.9 all-to-all-start.4
  1151.5 114.8 %all-gather.18.cloned.1.call-start = ((), (), s32[]{:S(2)}) async-start(), calls=%async_computation.16 | async-start | bytes 11141120 | tf_op jit(solution)/shard_map/all_gather | solution.py:349
  1151.6 16.0 copy-start.42
  1151.6 16.0 copy-start.44
  1163.6 176.5 %all-gather.20.cloned.1.call-start = ((), (), s32[]{:S(2)}) async-start(), calls=%async_computation.17 | async-start | bytes 8912896 | tf_op jit(solution)/shard_map/all_gather | solution.py:350
  1164.2 421.8 %all-gather.22.cloned.1.call-start = ((), (), s32[]{:S(2)}) async-start(), calls=%async_computation.18 | async-start | bytes 49020928 | tf_op jit(solution)/shard_map/all_gather | solution.py:351
  1167.6 25.9 %copy-start.14 = (bf16[16,128,128]{1,2,0:T(8,128)(2,1)S(1)}, bf16[16,128,128]{1,2,0:T(8,128)(2,1)}, u32[]{:S(2)}) copy-start(bf16[16,128,128]{1,2,0:T(8,128)(2,1)} %copy-done.13) | copy-start | bytes 1572868
  1167.6 557.5 %all-gather.24.cloned.1.call-start = ((), (), s32[]{:S(2)}) async-start(), calls=%async_computation.19 | async-start | bytes 24510464 | tf_op jit(solution)/shard_map/all_gather | solution.py:352
  1168.4 40.6 %copy-start.19 = (bf16[128,2048]{1,0:T(8,128)(2,1)S(1)}, bf16[128,2048]{1,0:T(8,128)(2,1)}, u32[]{:S(2)}) copy-start(bf16[128,2048]{1,0:T(8,128)(2,1)} %copy-done.18) | copy-start | bytes 1572868
  1169.0 56.2 %copy-start.32 = (bf16[16,128,128]{1,2,0:T(8,128)(2,1)S(1)}, bf16[16,128,128]{1,2,0:T(8,128)(2,1)}, u32[]{:S(2)}) copy-start(bf16[16,128,128]{1,2,0:T(8,128)(2,1)} %copy-done.31) | copy-start | bytes 1572868
  1169.1 56.2 %copy-start.43 = (bf16[128,4,64]{0,2,1:T(8,128)(2,1)S(1)}, bf16[128,4,64]{0,2,1:T(8,128)(2,1)}, u32[]{:S(2)}) copy-start(bf16[128,4,64]{0,2,1:T(8,128)(2,1)} %copy-done.42) | copy-start | bytes 196612
  1169.1 56.2 %copy-start.45 = (bf16[128,4,64]{0,2,1:T(8,128)(2,1)S(1)}, bf16[128,4,64]{0,2,1:T(8,128)(2,1)}, u32[]{:S(2)}) copy-start(bf16[128,4,64]{0,2,1:T(8,128)(2,1)} %copy-done.44) | copy-start | bytes 196612
  1169.1 56.2 %copy-start.49 = (f32[2048,1]{0,1:T(1,128)S(1)}, f32[2048,1]{0,1:T(1,128)}, u32[]{:S(2)}) copy-start(f32[2048,1]{0,1:T(1,128)} %copy-done.48) | copy-start | bytes 24580
  1169.9 19.4 %all-to-all-start.6 = ((bf16[16,128,128]{1,2,0:T(8,128)(2,1)}), bf16[16,128,128]{1,2,0:T(8,128)(2,1)S(1)}, u32[]{:S(2)}, u32[]{:S(2)}) async-start(bf16[16,128,128]{1,2,0:T(8,128)(2,1)} %bitcast.310), calls=%async_computation.6 | async-start | bytes 1048576 | tf_op jit(solution)/shard_map/all_to_all | solution.py:308
  1189.4 14.9 all-to-all-start.9
  1204.2 15.9 all-to-all-start.7
  1220.2 14.2 copy-start.33
  1220.2 16.3 all-to-all-start.8
  1236.5 12.8 all-to-all-start.10
  1242.4 608.6 %reduce-scatter.4.cloned.1.call-start = ((), (), s32[]{:S(2)}) async-start(), calls=%async_computation.20 | async-start | bytes 6230016
  1738.4 8.4 copy-start.38
  1738.4 9.8 copy-start.29
  1766.7 23.5 %copy-start.3 = (f32[128,2048]{1,0:T(8,128)S(1)}, f32[128,2048]{1,0:T(8,128)}, u32[]{:S(2)}) copy-start(f32[128,2048]{1,0:T(8,128)} %copy-done.2) | copy-start | bytes 3145732
  1766.7 23.5 %copy-start.10 = (bf16[128,5632]{1,0:T(8,128)(2,1)S(1)}, bf16[128,5632]{1,0:T(8,128)(2,1)}, u32[]{:S(2)}) copy-start(bf16[128,5632]{1,0:T(8,128)(2,1)} %get-tuple-element.460) | copy-start | bytes 4325380
  1790.2 13.2 copy-start.60
  1790.2 13.2 copy-start.12
  1790.2 13.2 copy-start.36
  1790.2 13.2 copy-start.47
  1790.2 13.2 copy-start.52
  1790.2 13.2 copy-start.56
  1851.0 12.8 slice-start
  1884.1 10.2 copy-start.8
  1910.8 11.3 copy-start.16
  1910.8 11.3 copy-start.17
  1922.1 11.7 copy-start.57
  1922.1 11.7 copy-start.58
  1922.1 11.7 copy-start.59
  (25 other events, 123.8 us)
Sparse Core Ops, SparseCore 0:
  10.3 209.4 all-gather.9
  222.2 205.9 all-gather.11
  430.4 258.8 all-gather.13
  691.5 224.0 all-gather.15
  1163.8 102.5 all-gather.17
  1269.2 70.9 all-gather.19
  1342.6 243.4 all-gather.21
  1588.5 136.5 all-gather.23
  1737.8 113.1 reduce-scatter.3
where the time goes:
time: 1950 us; the launch traced here: 1940 us
  waiting for transfers between devices  1150 us (59%)
  matrix products  229 us (12%)
  blocking collectives  179 us (9%)
  local copies, waits for them, and re-layouts  164 us (8%)
  other arithmetic  123 us (6%)
  starting transfers between devices  57.9 us (3%)
  loops' own time  24 us (1%)
    all_gather x1, waiting for transfers between devices, local(): lax.all_gather(low_shards[2], ('dp', 'seq'), axis=0, tiled=True)  256 us
    all_gather x1, waiting for transfers between devices, local(): lax.all_gather(gate_up_grad, 'seq', axis=0, tiled=True)  240 us
    all_gather x1, waiting for transfers between devices, local(): lax.all_gather(low_shards[3], ('dp', 'seq'), axis=0, tiled=True)  206 us
    all_gather x1, blocking collectives, local(): lax.all_gather(low_shards[4], ('dp', 'seq'), axis=0, tiled=True)  179 us
    all_gather x1, waiting for transfers between devices, local(): lax.all_gather(hidden, 'seq', axis=0, tiled=True)  119 us
    all_gather x1, waiting for transfers between devices, local(): lax.all_gather(low_shards[1], ('dp', 'seq'), axis=0, tiled=True)  102 us
    all_gather x1, waiting for transfers between devices, local(): lax.all_gather(attn_grad, 'seq', axis=0, tiled=True)  65.4 us
    unnamed x143, local copies, waits for them, and re-layouts  55 us
  transfers between devices with their start and end apart: 20, of which 19 were waited for; matrix products, arithmetic and copies ran while one was open for 12% of the time, Pallas kernels for 0%

commit v1 on v0

v1 whole, which is shorter than its diff:
```python
import functools
import math

import jax
import jax.numpy as jnp
import numpy as np
from jax import lax
from jax.experimental import pallas as pl
from jax.experimental.pallas import tpu as pltpu
from jax.sharding import Mesh
from jax.sharding import PartitionSpec as P

D = 2048
HEAD = 64
FF = 5632
STEP = 10
SEG = FF // 8
QKV = 512

norm_eps = 1e-05
rope_base = 10000.0
mask_fill = -1e30
beta_one = 0.9
beta_two = 0.95
adam_eps = 1e-08
decay_rate = 0.1
rate_matrix = 0.08
rate_gain = 0.8

BF = jnp.bfloat16
F32 = jnp.float32
MESH = pl.DeviceIdType.MESH
ANY = pl.BlockSpec(memory_space=pl.ANY)
VM = pl.BlockSpec(memory_space=pltpu.VMEM)
VLIMIT = 56 * 2**20


def shaped(*shape, dtype=BF):
    return jax.ShapeDtypeStruct(shape, dtype)


class Place:
    def __init__(self):
        self.x, self.zlo, self.y = (lax.axis_index(a) for a in ("x", "zlo", "y"))
        self.zhi, self.core = lax.axis_index("zhi"), lax.axis_index("core")
        self.z = self.zhi * 2 + self.zlo
        self.t = self.y * 2 + self.core
        self.sib = {"core": 1 - self.core}
        self.right = {"y": lax.rem(self.y + 1, 4)}
        self.left = {"y": lax.rem(self.y + 3, 4)}
        self.zpart = {"zhi": 1 - self.zhi}

    def xs(self, step):
        return lax.rem(self.x + step, 4)

    def ys(self, step):
        return lax.rem(self.y + step, 4)

    def zs(self, step):
        z = lax.rem(self.z + step, 4)
        return lax.div(z, 2), lax.rem(z, 2)

    def xpeers(self):
        return [{"x": self.xs(i)} for i in (1, 2, 3)]

    def zpeers(self):
        out = []
        for i in (1, 2, 3):
            zhi, zlo = self.zs(i)
            out.append({"zhi": zhi, "zlo": zlo})
        return out

    def tpeers(self):
        return [
            {"y": self.ys(dy), "core": lax.rem(self.core + dc, 2)}
            for dy in range(4)
            for dc in range(2)
            if (dy, dc) != (0, 0)
        ]

    def plane(self):
        out = []
        for dx in range(4):
            for dz in range(4):
                for dc in range(2):
                    if (dx, dz, dc) != (0, 0, 0):
                        zhi, zlo = self.zs(dz)
                        out.append(
                            {"x": self.xs(dx), "zhi": zhi, "zlo": zlo, "core": lax.rem(self.core + dc, 2)}
                        )
        return out


def greet(peers):
    barrier = pltpu.get_barrier_semaphore()
    for peer in peers:
        pl.semaphore_signal(barrier, inc=1, device_id=peer, device_id_type=MESH)
    pl.semaphore_wait(barrier, len(peers))


class Net:
    def __init__(self, send, recv, local):
        self.send, self.recv, self.loc = send, recv, local
        self.n = 0
        self.m = 0

    def block(self, count):
        first = self.n
        self.n += count
        return first

    def make(self, src, dst, peer, at=None):
        if at is None:
            at = self.block(1)
        return pltpu.make_async_remote_copy(
            src, dst, self.send.at[at], self.recv.at[at], device_id=peer, device_id_type=MESH
        )

    def go(self, src, dst, peer, at=None):
        copy = self.make(src, dst, peer, at)
        copy.start()
        return copy

    def local(self, src, dst):
        copy = pltpu.make_async_copy(src, dst, self.loc.at[self.m])
        self.m += 1
        copy.start()
        return copy


def sems(remote, local):
    return [
        pltpu.SemaphoreType.DMA((remote,)),
        pltpu.SemaphoreType.DMA((remote,)),
        pltpu.SemaphoreType.DMA((max(local, 1),)),
    ]


class Gather:
    def __init__(self, net, pos, src, out):
        self.net, self.pos, self.src, self.out = net, pos, src, out

    def start(self):
        net, pos, src = self.net, self.pos, self.src
        mine = self.out.at[pos.t]
        lo, hi = pl.ds(0, 64), pl.ds(64, 64)
        self.own = net.local(src, mine)
        self.r = [net.go(src.at[lo], mine.at[lo], pos.right), None]
        self.l = [net.go(src.at[hi], mine.at[hi], pos.left), None]
        self.r[1] = net.go(src.at[hi], mine.at[hi], pos.right)
        self.l[1] = net.go(src.at[lo], mine.at[lo], pos.left)
        self.s = [net.go(src, mine, pos.sib)]

    def step(self):
        net, pos, out = self.net, self.pos, self.out
        lo, hi = pl.ds(0, 64), pl.ds(64, 64)
        from_left = out.at[pos.ys(3) * 2 + pos.core]
        from_right = out.at[pos.ys(1) * 2 + pos.core]
        self.r[0].wait_recv()
        self.r2 = net.go(from_left.at[lo], from_left.at[lo], pos.right)
        self.l[0].wait_recv()
        self.l2 = net.go(from_right.at[hi], from_right.at[hi], pos.left)
        self.r[1].wait_recv()
        self.s.append(net.go(from_left, from_left, pos.sib))
        self.l[1].wait_recv()
        self.s.append(net.go(from_right, from_right, pos.sib))

    def last(self):
        net, pos = self.net, self.pos
        far = self.out.at[pos.ys(2) * 2 + pos.core]
        lo, hi = pl.ds(0, 64), pl.ds(64, 64)
        self.r2.wait_recv()
        self.s.append(net.go(far.at[lo], far.at[lo], pos.sib))
        self.l2.wait_recv()
        self.s.append(net.go(far.at[hi], far.at[hi], pos.sib))

    def finish(self):
        for copy in self.r + self.l + [self.r2, self.l2]:
            copy.wait_send()
        for copy in self.s:
            copy.wait()
        self.own.wait()


GATHER_SEMS = 11


class Scatter:
    def __init__(self, net, pos, part, scratch):
        self.net, self.pos, self.part = net, pos, part
        self.sib, self.opp, self.nb, self.far, self.near = scratch

    def start(self):
        net, pos = self.net, self.pos
        self.c = {}
        for dy in (2, 1, 3, 0):
            self.c[dy] = net.go(
                self.part.at[pos.ys(dy) * 2 + 1 - pos.core], self.sib.at[dy], pos.sib
            )

    def _add(self, dst, dy, rows):
        pos = self.pos
        one = self.part[pos.ys(dy) * 2 + pos.core, rows].astype(F32)
        dst[rows] = (one + self.sib[dy, rows].astype(F32)).astype(BF)

    def step(self):
        net, pos = self.net, self.pos
        lo, hi = pl.ds(0, 64), pl.ds(64, 64)
        self.c[2].wait_recv()
        self._add(self.far, 2, lo)
        self.f0 = net.go(self.far.at[lo], self.opp.at[0], pos.right)
        self._add(self.far, 2, hi)
        self.f1 = net.go(self.far.at[hi], self.opp.at[1], pos.left)
        self.c[1].wait_recv()
        self._add(self.near.at[0], 1, hi)
        self.r1 = net.go(self.near.at[0, hi], self.nb.at[0, hi], pos.right)
        self.c[3].wait_recv()
        self._add(self.near.at[1], 3, lo)
        self.l0 = net.go(self.near.at[1, lo], self.nb.at[1, lo], pos.left)
        self._add(self.near.at[0], 1, lo)
        self._add(self.near.at[1], 3, hi)

    def last(self):
        net, pos = self.net, self.pos
        lo, hi = pl.ds(0, 64), pl.ds(64, 64)
        self.f0.wait_recv()
        self.near[0, lo] = (self.near[0, lo].astype(F32) + self.opp[0].astype(F32)).astype(BF)
        self.r0 = net.go(self.near.at[0, lo], self.nb.at[0, lo], pos.right)
        self.f1.wait_recv()
        self.near[1, hi] = (self.near[1, hi].astype(F32) + self.opp[1].astype(F32)).astype(BF)
        self.l1 = net.go(self.near.at[1, hi], self.nb.at[1, hi], pos.left)

    def arrive(self):
        for copy in (self.r1, self.l0, self.r0, self.l1, self.c[0]):
            copy.wait_recv()

    def total(self, rows):
        pos = self.pos
        out = self.part[pos.t, rows].astype(F32) + self.sib[0, rows].astype(F32)
        return out + self.nb[0, rows].astype(F32) + self.nb[1, rows].astype(F32)

    def finish(self):
        for copy in (self.f0, self.f1, self.r0, self.r1, self.l0, self.l1):
            copy.wait_send()
        for copy in self.c.values():
            copy.wait_send()


SCATTER_SEMS = 10


def scatter_scratch():
    return [
        pltpu.VMEM((4, 128, D), BF),
        pltpu.VMEM((2, 64, D), BF),
        pltpu.VMEM((2, 128, D), BF),
        pltpu.VMEM((128, D), BF),
        pltpu.VMEM((2, 128, D), BF),
    ]


def first_kernel(
    n_ref, wq_ref, wr_ref, nf_ref, wqf_ref, ra_ref, rb_ref, own_ref, send, recv, local
):
    pos, net = Place(), Net(send, recv, local)
    tpeers, xpeers, zpeers = pos.tpeers(), pos.xpeers(), pos.zpeers()
    greet(tpeers + xpeers + zpeers)
    x, y, zlo, zhi, core = pos.x, pos.y, pos.zlo, pos.zhi, pos.core
    low, high = pl.ds(0, 2), pl.ds(2, 2)

    small = []
    for peer in tpeers:
        t = peer["y"] * 2 + peer["core"]
        small.append(net.go(wq_ref.at[t], wqf_ref.at[x, zlo, y, zhi, core], peer))
    mine = net.local(wq_ref.at[pos.t], wqf_ref.at[x, zlo, y, zhi, core])
    gather = Gather(net, pos, n_ref, nf_ref)
    gather.start()
    large = []
    for peer in tpeers:
        t = peer["y"] * 2 + peer["core"]
        large.append(net.go(wr_ref.at[t], own_ref.at[:, y, core], peer))
    mine_large = net.local(wr_ref.at[pos.t], own_ref.at[:, y, core])

    mine.wait()
    for copy in small:
        copy.wait_recv()
    one = []
    for peer in xpeers:
        part = wqf_ref.at[x, zlo, low, zhi]
        one.append(net.go(part, part, peer))
    for peer in zpeers:
        part = wqf_ref.at[x, zlo, high, zhi]
        one.append(net.go(part, part, peer))

    gather.step()

    for copy in one:
        copy.wait_recv()
    two = []
    for peer in zpeers:
        part = wqf_ref.at[:, zlo, low, zhi]
        two.append(net.go(part, part, peer))
    for peer in xpeers:
        part = wqf_ref.at[x, :, high, :]
        two.append(net.go(part, part, peer))

    mine_large.wait()
    for copy in large:
        copy.wait_recv()
    three = []
    for peer in xpeers:
        three.append(net.go(own_ref.at[:, low], ra_ref.at[:, x], peer))
    for peer in zpeers:
        three.append(net.go(own_ref.at[:, high], rb_ref.at[:, zlo, :, zhi], peer))
    keep = [
        net.local(own_ref.at[:, low], ra_ref.at[:, x]),
        net.local(own_ref.at[:, high], rb_ref.at[:, zlo, :, zhi]),
    ]

    gather.last()
    gather.finish()
    for copy in small + large + one:
        copy.wait_send()
    for copy in two + three:
        copy.wait()
    for copy in keep:
        copy.wait()


def run_first(normed, wq_blocks, wr_blocks):
    return pl.pallas_call(
        first_kernel,
        out_shape=(
            shaped(8, 128, D),
            shaped(4, 2, 4, 2, 2, 16, QKV),
            shaped(3, 4, 2, 2, 16, SEG),
            shaped(3, 2, 2, 2, 2, 16, SEG),
        ),
        in_specs=[VM, ANY, ANY],
        out_specs=(VM, ANY, ANY, ANY),
        scratch_shapes=[pltpu.VMEM((3, 4, 2, 16, SEG), BF)] + sems(7 + 7 + 18 + GATHER_SEMS, 6),
        compiler_params=pltpu.CompilerParams(
            collective_id=0, has_side_effects=True, vmem_limit_bytes=VLIMIT
        ),
        name="first",
    )(normed, wq_blocks, wr_blocks)


def dot_nt(a, b):
    return lax.dot_general(a, b, (((1,), (1,)), ((), ())), preferred_element_type=F32)


def dot_tn(a, b):
    return lax.dot_general(a, b, (((0,), (0,)), ((), ())), preferred_element_type=F32)


def dot_nn(a, b):
    return lax.dot_general(a, b, (((1,), (0,)), ((), ())), preferred_element_type=F32)


def first_half_mask(shape):
    return (lax.broadcasted_iota(jnp.int32, shape, 1) & 63) < 32


def turn(u, cos, sin):
    rot = jnp.where(first_half_mask(u.shape), -pltpu.roll(u, 96, 1), pltpu.roll(u, 32, 1))
    return u * cos + rot * sin


def turn_back(u, cos, sin):
    v = u * sin
    rot = jnp.where(first_half_mask(u.shape), pltpu.roll(v, 96, 1), -pltpu.roll(v, 32, 1))
    return u * cos + rot


def lane_first(shape):
    return lax.broadcasted_iota(jnp.int32, shape, 1) < 64


def causal(zhi):
    key = lax.broadcasted_iota(jnp.int32, (512, 512), 0)
    query = (lax.broadcasted_iota(jnp.int32, (512, 512), 1) & 255) + zhi * 256
    return key <= query


class Spread:
    def __init__(self, net, pos, ra, rb, outs):
        self.net, self.pos, self.ra, self.rb, self.outs = net, pos, ra, rb, outs

    def start(self):
        net, pos = self.net, self.pos
        x, zlo, zhi = pos.x, pos.zlo, pos.zhi
        low, high = pl.ds(0, 2), pl.ds(2, 2)
        self.copies, self.keep = [], []
        for i, out in self.outs:
            part_a, part_b = out.at[:, zlo, low, zhi], out.at[x, :, high, :]
            src_a, src_b = self.ra.at[i], self.rb.at[i]
            for za, xb in zip(pos.zpeers(), pos.xpeers()):
                self.copies.append(net.go(src_a, part_a, za))
                self.copies.append(net.go(src_b, part_b, xb))
            self.keep += [net.local(src_a, part_a), net.local(src_b, part_b)]

    def finish(self):
        for copy in self.copies + self.keep:
            copy.wait()


class OutRows:
    def __init__(self, net, pos, src, out):
        self.net, self.pos, self.src, self.out = net, pos, src, out
        self.base = net.block(32)

    def _pairs(self):
        pos = self.pos
        for dx in range(4):
            for dz in range(4):
                yield dx, dz, pos.xs(dx), pos.zs(dz)

    def start(self):
        pos, net = self.pos, self.net
        half = lax.div(pos.x, 2)
        dst = self.out.at[lax.rem(pos.x, 2) * 2 + pos.zlo, pos.zhi, pos.core]
        for dx, dz, x, (zhi, zlo) in self._pairs():
            peer = {"x": x, "zhi": zhi, "zlo": zlo, "core": half}
            at = self.base + (dx * 4 + dz) * 2 + pos.core
            if (dx, dz) == (0, 0):

                @pl.when(half == pos.core)
                def _():
                    pltpu.make_async_copy(self.src, dst, net.loc.at[net.loc.shape[0] - 1]).start()

                @pl.when(half != pos.core)
                def _():
                    net.make(self.src, dst, peer, at).start()
            else:
                net.make(self.src, dst, peer, at).start()

    def finish(self):
        pos, net = self.pos, self.net
        half = lax.div(pos.x, 2)
        dst = self.out.at[lax.rem(pos.x, 2) * 2 + pos.zlo, pos.zhi, pos.core]
        for dx, dz, x, (zhi, zlo) in self._pairs():
            peer = {"x": x, "zhi": zhi, "zlo": zlo, "core": half}
            at = self.base + (dx * 4 + dz) * 2 + pos.core
            first = (dx, dz) == (0, 0)
            if first:

                @pl.when(half == pos.core)
                def _():
                    pltpu.make_async_copy(self.src, dst, net.loc.at[net.loc.shape[0] - 1]).wait()

                @pl.when(half != pos.core)
                def _():
                    net.make(self.src, dst, peer, at).wait_send()
            else:
                net.make(self.src, dst, peer, at).wait_send()
            back = lax.rem(pos.x + 4 - dx, 4)

            @pl.when(lax.div(back, 2) == pos.core)
            def _():
                for core in range(2):
                    slot = self.base + (dx * 4 + dz) * 2 + core
                    if first:

                        @pl.when(pos.core != core)
                        def _():
                            net.make(self.src, dst, peer, slot).wait_recv()
                    else:
                        net.make(self.src, dst, peer, slot).wait_recv()


def attend_kernel(
    qkv_ref, cos_ref, sin_ref, wout_ref, ra_ref, rb_ref, cot_ref,
    o_ref, lse_ref, q_ref, kv_ref, wg_ref, wu_ref, wd_ref, wo_ref, cotf_ref,
    k_ref, v_ref, send, recv, local,
):
    pos, net = Place(), Net(send, recv, local)
    zhi = pos.zhi
    greet(pos.plane() + [pos.right, pos.left])
    gather = Gather(net, pos, cot_ref, cotf_ref)
    spread = Spread(net, pos, ra_ref, rb_ref, [(2, wd_ref), (0, wg_ref), (1, wu_ref)])
    rows = OutRows(net, pos, wout_ref, wo_ref)

    swap = net.block(4)
    for j in range(4):
        r = pl.ds(j * 256, 256)
        cos, sin = cos_ref[r], sin_ref[r]
        for c in range(2):
            kv = qkv_ref[r, 256 + c * 128 : 384 + c * 128].astype(F32)
            mixed = jnp.where(lane_first(kv.shape), turn(kv, cos, sin), kv)
            kv_ref[j, zhi, :, c * 128 : (c + 1) * 128] = mixed.astype(BF)
        net.go(kv_ref.at[j, zhi], kv_ref.at[j, zhi], pos.zpart, swap + j)
    rows.start()
    spread.start()
    gather.start()
    for j in range(4):
        r = pl.ds(j * 256, 256)
        cos, sin = cos_ref[r], sin_ref[r]
        for c in range(2):
            q = turn(qkv_ref[r, c * 128 : (c + 1) * 128].astype(F32), cos, sin)
            q = q.astype(BF) * jnp.asarray(HEAD**-0.5, BF)
            q_ref[j, c, 0:256] = q[:, 0:64]
            q_ref[j, c, 256:512] = q[:, 64:128]

    def update(c, key_at, query, state, mask):
        top, norm, acc = state
        s = dot_nt(k_ref[c, key_at], query)
        if mask is not None:
            s = jnp.where(mask, s, mask_fill)
        new = jnp.maximum(top, jnp.max(s, axis=0, keepdims=True))
        p = jnp.exp(s - new)
        keep = jnp.exp(top - new)
        norm = norm * keep + jnp.sum(p, axis=0, keepdims=True)
        acc = acc * keep + dot_tn(v_ref[c, key_at], p.astype(BF))
        return new, norm, acc

    def block(qb, _):
        part = kv_ref.at[qb, zhi]
        net.make(part, part, pos.zpart, swap + qb).wait_recv()
        kv = kv_ref[qb].reshape(512, 256)
        for c in range(2):
            k_ref[c, qb] = kv[:, c * 128 : c * 128 + 64]
            v_ref[c, qb] = kv[:, c * 128 + 64 : c * 128 + 128]
        mask = causal(zhi)
        state = []
        for c in range(2):
            zero = (
                jnp.full((1, 512), mask_fill, F32),
                jnp.zeros((1, 512), F32),
                jnp.zeros((64, 512), F32),
            )
            state.append(update(c, qb, q_ref[qb, c], zero, mask))

        def more(j, held):
            return tuple(update(c, j, q_ref[qb, c], held[c], None) for c in range(2))

        state = lax.fori_loop(0, qb, more, tuple(state))
        for c in range(2):
            top, norm, acc = state[c]
            lse_ref[qb, c] = top + jnp.log(norm)
            out = (acc / norm).T
            pair = jnp.concatenate([out[0:256], out[256:512]], axis=1)
            o_ref[qb, :, c * 128 : (c + 1) * 128] = pair.astype(BF)
        return 0

    block(0, 0)
    gather.step()
    lax.fori_loop(1, 3, block, 0)
    gather.last()
    block(3, 0)
    gather.finish()
    spread.finish()
    rows.finish()
    for j in range(4):
        part = kv_ref.at[j, zhi]
        net.make(part, part, pos.zpart, swap + j).wait_send()


def run_attend(qkv, cos, sin, wout, ra, rb, cot):
    full = shaped(4, 2, 4, 2, 2, 16, SEG)
    return pl.pallas_call(
        attend_kernel,
        out_shape=(
            shaped(4, 256, 256),
            shaped(4, 2, 1, 512, dtype=F32),
            shaped(4, 2, 512, 64),
            shaped(4, 2, 256, 256),
            full,
            full,
            full,
            shaped(4, 2, 2, 16, D),
            shaped(8, 128, D),
        ),
        in_specs=[VM, VM, VM, ANY, ANY, ANY, ANY],
        out_specs=(VM, VM, VM, VM, ANY, ANY, ANY, ANY, ANY),
        scratch_shapes=[pltpu.VMEM((2, 4, 512, 64), BF), pltpu.VMEM((2, 4, 512, 64), BF)]
        + sems(4 + 18 + 32 + GATHER_SEMS, 9),
        compiler_params=pltpu.CompilerParams(
            collective_id=1, has_side_effects=True, vmem_limit_bytes=VLIMIT
        ),
        name="attend",
    )(qkv, cos, sin, wout, ra, rb, cot)


def mid_kernel(
    part_ref, tok_ref, resid_ref, full_ref, a, b, c, d, e, blk, send, recv, local
):
    pos, net = Place(), Net(send, recv, local)
    greet([pos.sib, pos.right, pos.left])
    sc = Scatter(net, pos, part_ref, (a, b, c, d, e))
    sc.start()
    sc.step()
    sc.last()
    sc.arrive()

    @pl.loop(0, 8)
    def _(i):
        rows = pl.ds(pl.multiple_of(i * 16, 16), 16)
        r = sc.total(rows) + tok_ref[rows].astype(F32)
        resid_ref[rows] = r
        inv = lax.rsqrt(jnp.mean(r * r, axis=-1, keepdims=True) + norm_eps)
        blk[rows] = (r * inv).astype(BF)

    gather = Gather(net, pos, blk, full_ref)
    gather.start()
    sc.finish()
    gather.step()
    gather.last()
    gather.finish()


def run_mid(part, tok):
    return pl.pallas_call(
        mid_kernel,
        out_shape=(shaped(128, D, dtype=F32), shaped(8, 128, D)),
        in_specs=[VM, VM],
        out_specs=(VM, VM),
        scratch_shapes=scatter_scratch()
        + [pltpu.VMEM((128, D), BF)]
        + sems(SCATTER_SEMS + GATHER_SEMS, 1),
        compiler_params=pltpu.CompilerParams(
            collective_id=2, has_side_effects=True, vmem_limit_bytes=VLIMIT
        ),
        name="mid",
    )(part, tok)


def norm_back(t, r, back):
    inv = lax.rsqrt(jnp.mean(r * r, axis=-1, keepdims=True) + norm_eps)
    normed = r * inv
    return back + inv * (t - normed * jnp.mean(t * normed, axis=-1, keepdims=True))


def back_kernel(
    part_ref, resid_ref, cot_ref, dmid_ref, full_ref, a, b, c, d, e, blk, send, recv, local
):
    pos, net = Place(), Net(send, recv, local)
    greet([pos.sib, pos.right, pos.left])
    sc = Scatter(net, pos, part_ref, (a, b, c, d, e))
    sc.start()
    sc.step()
    sc.last()
    sc.arrive()

    @pl.loop(0, 8)
    def _(i):
        rows = pl.ds(pl.multiple_of(i * 16, 16), 16)
        dmid = norm_back(sc.total(rows), resid_ref[rows], cot_ref[rows].astype(F32))
        dmid_ref[rows] = dmid
        blk[rows] = dmid.astype(BF)

    gather = Gather(net, pos, blk, full_ref)
    gather.start()
    sc.finish()
    gather.step()
    gather.last()
    gather.finish()


def run_back(part, resid, cot):
    return pl.pallas_call(
        back_kernel,
        out_shape=(shaped(128, D, dtype=F32), shaped(8, 128, D)),
        in_specs=[VM, VM, VM],
        out_specs=(VM, VM),
        scratch_shapes=scatter_scratch()
        + [pltpu.VMEM((128, D), BF)]
        + sems(SCATTER_SEMS + GATHER_SEMS, 1),
        compiler_params=pltpu.CompilerParams(
            collective_id=3, has_side_effects=True, vmem_limit_bytes=VLIMIT
        ),
        name="back",
    )(part, resid, cot)


class Fold:
    def __init__(self, net, pos, src, scratch):
        self.net, self.pos, self.src = net, pos, src
        self.ra, self.rb, self.sa, self.sb, self.ta, self.tb = scratch

    def start(self):
        net, pos, src = self.net, self.pos, self.src
        low, high = pl.ds(0, 2), pl.ds(2, 2)
        self.one = []
        for i, (za, xb) in enumerate(zip(pos.zpeers(), pos.xpeers())):
            self.one.append(net.go(src.at[:, za["zlo"], low, za["zhi"]], self.ra.at[i], za))
            self.one.append(net.go(src.at[xb["x"], :, high, :], self.rb.at[i], xb))
        self.keep = [
            net.local(src.at[:, pos.zlo, low, pos.zhi], self.sa),
            net.local(src.at[pos.x, :, high, :], self.sb),
        ]

    def step(self):
        net, pos = self.net, self.pos
        for copy in self.keep:
            copy.wait()
        for copy in self.one:
            copy.wait_recv()

        @pl.loop(0, 4)
        def _(i):
            for j in range(2):
                here = self.sa[i, j].astype(F32)
                for k in range(3):
                    here += self.ra[k, i, j].astype(F32)
                self.sa[i, j] = here.astype(BF)
            lo, hi = lax.div(i, 2), lax.rem(i, 2)
            for j in range(2):
                here = self.sb[lo, j, hi].astype(F32)
                for k in range(3):
                    here += self.rb[k, lo, j, hi].astype(F32)
                self.sb[lo, j, hi] = here.astype(BF)

        self.two = []
        for i, (za, xb) in enumerate(zip(pos.zpeers(), pos.xpeers())):
            self.two.append(net.go(self.sa.at[xb["x"]], self.ta.at[i], xb))
            self.two.append(net.go(self.sb.at[za["zlo"], :, za["zhi"]], self.tb.at[i], za))

    def finish(self, out):
        pos = self.pos
        for copy in self.two:
            copy.wait_recv()
        for j in range(2):
            here = self.sa[pos.x, j].astype(F32)
            for k in range(3):
                here += self.ta[k, j].astype(F32)
            out[j] = here.astype(BF)
            here = self.sb[pos.zlo, j, pos.zhi].astype(F32)
            for k in range(3):
                here += self.tb[k, j].astype(F32)
            out[2 + j] = here.astype(BF)
        for copy in self.one + self.two:
            copy.wait_send()


FOLD_SEMS = 12


def fold_scratch(cols):
    return [
        pltpu.VMEM((3, 4, 2, 2, 16, cols), BF),
        pltpu.VMEM((3, 2, 2, 2, 2, 16, cols), BF),
        pltpu.VMEM((4, 2, 2, 16, cols), BF),
        pltpu.VMEM((2, 2, 2, 2, 16, cols), BF),
        pltpu.VMEM((3, 2, 2, 16, cols), BF),
        pltpu.VMEM((3, 2, 2, 16, cols), BF),
    ]


class OutFold:
    def __init__(self, net, pos, src, land):
        self.net, self.pos, self.src, self.land = net, pos, src, land
        self.base = net.block(32)

    def _targets(self):
        for xh in range(2):
            for dz in range(4):
                for core in range(2):
                    yield xh, dz, core

    def _copy(self, xh, dz, core):
        pos, net = self.pos, self.net
        zhi, zlo = pos.zs(dz)
        x = pos.core * 2 + xh
        peer = {"x": x, "zhi": zhi, "zlo": zlo, "core": core}
        dx = lax.rem(pos.x + 4 - x, 4)
        src = self.src.at[xh * 2 + zlo, zhi, core]
        slot = dx * 4 + (4 - dz) % 4
        return peer, src, slot

    def start(self):
        pos, net = self.pos, self.net
        for n, (xh, dz, core) in enumerate(self._targets()):
            peer, src, slot = self._copy(xh, dz, core)

            def send(peer=peer, src=src, slot=slot, n=n):
                pltpu.make_async_remote_copy(
                    src, self.land.at[slot], net.send.at[self.base + n], net.recv.at[self.base + slot],
                    device_id=peer, device_id_type=MESH,
                ).start()

            if dz == 0:
                here = (pos.core * 2 + xh == pos.x) & (pos.core == core)

                @pl.when(here)
                def _(src=src):
                    pltpu.make_async_copy(src, self.land.at[0], net.loc.at[net.loc.shape[0] - 1]).start()

                @pl.when(jnp.logical_not(here))
                def _(send=send):
                    send()
            else:
                send()

    def finish(self, out):
        pos, net = self.pos, self.net
        for n, (xh, dz, core) in enumerate(self._targets()):
            peer, src, slot = self._copy(xh, dz, core)

            def sent(peer=peer, src=src, slot=slot, n=n):
                pltpu.make_async_remote_copy(
                    src, self.land.at[slot], net.send.at[self.base + n], net.recv.at[self.base + slot],
                    device_id=peer, device_id_type=MESH,
                ).wait_send()

            if dz == 0:
                here = (pos.core * 2 + xh == pos.x) & (pos.core == core)

                @pl.when(here)
                def _(src=src):
                    pltpu.make_async_copy(src, self.land.at[0], net.loc.at[net.loc.shape[0] - 1]).wait()

                @pl.when(jnp.logical_not(here))
                def _(sent=sent):
                    sent()
            else:
                sent()
        for slot in range(16):
            probe = pltpu.make_async_remote_copy(
                self.src.at[0, 0, 0], self.land.at[slot], net.send.at[self.base], net.recv.at[self.base + slot],
                device_id=pos.sib, device_id_type=MESH,
            )
            if slot == 0:

                @pl.when(lax.div(pos.x, 2) != pos.core)
                def _():
                    probe.wait_recv()
            else:
                probe.wait_recv()
        here = self.land[0].astype(F32)
        for slot in range(1, 16):
            here += self.land[slot].astype(F32)
        out[...] = here


def attend_back_kernel(
    q_ref, kv_ref, lse_ref, o_ref, do_ref, cos_ref, sin_ref, part_ref, resid_ref,
    gg_ref, gu_ref, gd_ref, go_ref,
    dqkv_ref, block_ref, fold_ref, fo_ref,
    k_ref, v_ref, do2_ref, delta_ref, dq_ref, dk_ref, dv_ref, send_ref, got_ref, mine_ref,
    *rest,
):
    pos = Place()
    folds, rest = rest[:18], rest[18:]
    land_ref, rest = rest[0], rest[1:]
    sc_scratch, rest = rest[:5], rest[5:]
    net = Net(*rest)
    zhi = pos.zhi
    greet(pos.plane() + [pos.right, pos.left])
    sc = Scatter(net, pos, part_ref, sc_scratch)
    fd = [Fold(net, pos, g, folds[i * 6 : i * 6 + 6]) for i, g in enumerate((gg_ref, gu_ref, gd_ref))]
    rows = OutFold(net, pos, go_ref, land_ref)
    for f in fd:
        f.start()
    sc.start()
    rows.start()

    for j in range(4):
        kv = kv_ref[j].reshape(512, 256)
        for c in range(2):
            k_ref[c, j] = kv[:, c * 128 : c * 128 + 64]
            v_ref[c, j] = kv[:, c * 128 + 64 : c * 128 + 128]
            cols = slice(c * 128, (c + 1) * 128)
            do = do_ref[j, :, cols]
            do2_ref[j, c, 0:256] = do[:, 0:64]
            do2_ref[j, c, 256:512] = do[:, 64:128]
            both = (do.astype(F32) * o_ref[j, :, cols].astype(F32)).T
            delta_ref[j, c] = jnp.concatenate(
                [
                    jnp.sum(both[0:64], axis=0, keepdims=True),
                    jnp.sum(both[64:128], axis=0, keepdims=True),
                ],
                axis=1,
            )
    dq_ref[...] = jnp.zeros_like(dq_ref)
    sc.step()

    swap = net.block(4)

    def pair(c, j, qb, mask):
        k, v, q, do = k_ref[c, j], v_ref[c, j], q_ref[qb, c], do2_ref[qb, c]
        p = jnp.exp(dot_nt(k, q) - lse_ref[qb, c])
        if mask is not None:
            p = jnp.where(mask, p, 0.0)
        ds = (p * (dot_nt(v, do) - delta_ref[qb, c])).astype(BF)
        dv = dot_nn(p.astype(BF), do)
        dk = dot_nn(ds, q)
        dq_ref[qb, c] += dot_tn(k, ds)
        return dk, dv

    def column(j, _):
        mask = causal(zhi)
        for c in range(2):
            dk, dv = pair(c, j, j, mask)
            dk_ref[c] = dk
            dv_ref[c] = dv

        def more(qb, _):
            for c in range(2):
                dk, dv = pair(c, j, qb, None)
                dk_ref[c] += dk
                dv_ref[c] += dv
            return 0

        lax.fori_loop(j + 1, 4, more, 0)
        both = jnp.concatenate([dk_ref[0], dv_ref[0], dk_ref[1], dv_ref[1]], axis=1)
        both = both.reshape(2, 256, 256)

        @pl.when(zhi == 0)
        def _():
            mine_ref[j] = both[0]
            send_ref[j] = both[1].astype(BF)

        @pl.when(zhi == 1)
        def _():
            mine_ref[j] = both[1]
            send_ref[j] = both[0].astype(BF)

        net.go(send_ref.at[j], got_ref.at[j], pos.zpart, swap + j)
        return 0

    column(0, 0)
    sc.last()
    for f in fd:
        f.step()
    lax.fori_loop(1, 4, column, 0)

    sc.arrive()

    @pl.loop(0, 8)
    def _(i):
        r = pl.ds(pl.multiple_of(i * 16, 16), 16)
        block_ref[r] = (sc.total(r) + resid_ref[r]).astype(BF)

    for j in range(4):
        r = pl.ds(j * 256, 256)
        cos, sin = cos_ref[r], sin_ref[r]
        for c in range(2):
            dq = dq_ref[j, c].T * HEAD**-0.5
            dq = jnp.concatenate([dq[0:256], dq[256:512]], axis=1)
            dqkv_ref[r, c * 128 : (c + 1) * 128] = turn_back(dq, cos, sin).astype(BF)
    for j in range(4):
        r = pl.ds(j * 256, 256)
        cos, sin = cos_ref[r], sin_ref[r]
        net.make(send_ref.at[j], got_ref.at[j], pos.zpart, swap + j).wait()
        for c in range(2):
            cols = slice(c * 128, (c + 1) * 128)
            dkv = mine_ref[j, :, cols] + got_ref[j, :, cols].astype(F32)
            dkv = jnp.where(lane_first(dkv.shape), turn_back(dkv, cos, sin), dkv)
            dqkv_ref[r, 256 + c * 128 : 384 + c * 128] = dkv.astype(BF)

    for i, f in enumerate(fd):
        f.finish(fold_ref.at[i])
    rows.finish(fo_ref)
    sc.finish()


def run_attend_back(q, kv, lse, o, do, cos, sin, part, resid, gg, gu, gd, go):
    return pl.pallas_call(
        attend_back_kernel,
        out_shape=(
            shaped(1024, QKV),
            shaped(128, D),
            shaped(3, 4, 2, 16, SEG),
            shaped(16, D, dtype=F32),
        ),
        in_specs=[VM] * 9 + [ANY] * 4,
        out_specs=(VM, VM, VM, VM),
        scratch_shapes=[
            pltpu.VMEM((2, 4, 512, 64), BF),
            pltpu.VMEM((2, 4, 512, 64), BF),
            pltpu.VMEM((4, 2, 512, 64), BF),
            pltpu.VMEM((4, 2, 1, 512), F32),
            pltpu.VMEM((4, 2, 64, 512), F32),
            pltpu.VMEM((2, 512, 64), F32),
            pltpu.VMEM((2, 512, 64), F32),
            pltpu.VMEM((4, 256, 256), BF),
            pltpu.VMEM((4, 256, 256), BF),
            pltpu.VMEM((4, 256, 256), F32),
        ]
        + fold_scratch(SEG) * 3
        + [pltpu.VMEM((16, 16, D), BF)]
        + scatter_scratch()
        + sems(4 + 3 * FOLD_SEMS + 32 + SCATTER_SEMS, 8),
        compiler_params=pltpu.CompilerParams(
            collective_id=4, has_side_effects=True, vmem_limit_bytes=VLIMIT
        ),
        name="attend_back",
    )(q, kv, lse, o, do, cos, sin, part, resid, gg, gu, gd, go)


def last_kernel(
    part_ref, tok_ref, dmid_ref, gq_ref, fold_ref, dtok_ref, outq_ref, outr_ref, sumq_ref, *rest
):
    pos = Place()
    fold_s, sc_scratch, rest = rest[:6], rest[6:11], rest[11:]
    net = Net(*rest)
    tpeers = pos.tpeers()
    greet(tpeers + pos.xpeers() + pos.zpeers())
    fd = Fold(net, pos, gq_ref, fold_s)
    sc = Scatter(net, pos, part_ref, sc_scratch)
    fd.start()
    sc.start()
    sc.step()
    ship = []
    for peer in tpeers:
        ship.append(net.go(fold_ref.at[:, peer["y"], peer["core"]], outr_ref.at[pos.t], peer))
    keep = [net.local(fold_ref.at[:, pos.y, pos.core], outr_ref.at[pos.t])]
    fd.step()
    sc.last()
    fd.finish(sumq_ref)
    for peer in tpeers:
        ship.append(net.go(sumq_ref.at[peer["y"], peer["core"]], outq_ref.at[pos.t], peer))
    keep.append(net.local(sumq_ref.at[pos.y, pos.core], outq_ref.at[pos.t]))
    sc.arrive()

    @pl.loop(0, 8)
    def _(i):
        rows = pl.ds(pl.multiple_of(i * 16, 16), 16)
        r = tok_ref[rows].astype(F32)
        dtok_ref[rows] = norm_back(sc.total(rows), r, dmid_ref[rows]).astype(BF)

    for copy in ship + keep:
        copy.wait()
    sc.finish()


def run_last(part, tok, dmid, gq, fold):
    return pl.pallas_call(
        last_kernel,
        out_shape=(shaped(128, D), shaped(8, 16, QKV), shaped(8, 3, 16, SEG)),
        in_specs=[VM, VM, VM, ANY, ANY],
        out_specs=(VM, ANY, ANY),
        scratch_shapes=[pltpu.VMEM((4, 2, 16, QKV), BF)]
        + fold_scratch(QKV)
        + scatter_scratch()
        + sems(FOLD_SEMS + SCATTER_SEMS + 14, 4),
        compiler_params=pltpu.CompilerParams(
            collective_id=5, has_side_effects=True, vmem_limit_bytes=VLIMIT
        ),
        name="last",
    )(part, tok, dmid, gq, fold)


def rope_tables():
    half = HEAD // 2
    freq = np.exp(np.arange(half, dtype=np.float32) * np.float32(-2.0 * math.log(rope_base) / HEAD))
    spots = np.arange(2048, dtype=np.float32).reshape(4, 2, 256).transpose(1, 0, 2).reshape(2, 1024)
    angles = (spots[:, :, None] * freq.astype(np.float32)).astype(np.float32)
    angles = np.concatenate([angles] * 4, axis=2)
    return np.cos(angles).astype(np.float32), np.sin(angles).astype(np.float32)


def adam(weight, gradient, first_moment, second, step_rate, decay_weight):
    first_new = beta_one * first_moment + (1.0 - beta_one) * gradient
    second_new = beta_two * second + (1.0 - beta_two) * gradient * gradient
    first_hat = first_new / (1.0 - beta_one**STEP)
    second_hat = second_new / (1.0 - beta_two**STEP)
    weight_new = weight - step_rate * (
        first_hat / (jnp.sqrt(second_hat) + adam_eps) + decay_weight * weight
    )
    return (first_new, second_new, weight_new)


def local(
    tokens, cotangent, w_qkv, w_out, w_gate_up, w_down_t, gains,
    first_qkv, second_qkv, first_out, second_out, first_gate_up, second_gate_up,
    first_down, second_down, first_gains, second_gains,
):
    tok, cot = tokens[0], cotangent[0]
    inputs = tok.astype(F32)
    inv = lax.rsqrt(jnp.mean(inputs * inputs, axis=-1, keepdims=True) + norm_eps)
    normed = (inputs * inv).astype(BF)

    gain = gains.astype(BF).astype(F32)
    low_qkv = w_qkv.astype(BF).astype(F32)
    low_gu = w_gate_up.astype(BF).astype(F32)
    qkv_g = (low_qkv * gain[:, 0:1]).astype(BF)
    gu_g = (low_gu * gain[:, 1:2]).astype(BF)
    q_cut = qkv_g[:, :D].reshape(16, 2, 4, 4, HEAD).transpose(3, 1, 0, 2, 4).reshape(4, 2, 16, 256)
    kv_cut = jnp.concatenate(
        [qkv_g[:, D : D + 256].reshape(16, 2, 2, HEAD), qkv_g[:, D + 256 :].reshape(16, 2, 2, HEAD)],
        axis=3,
    )
    kv_cut = kv_cut.transpose(1, 0, 2, 3).reshape(1, 2, 16, 256)
    wq_blocks = jnp.concatenate(
        [q_cut, jnp.broadcast_to(kv_cut, (4, 2, 16, 256))], axis=3
    ).reshape(8, 16, QKV)

    def cut(rows):
        return rows.reshape(16, 8, SEG).transpose(1, 0, 2)

    wr_blocks = jnp.stack(
        [cut(gu_g[:, :FF]), cut(gu_g[:, FF:]), cut(w_down_t.astype(BF))], axis=1
    )

    zhi = lax.axis_index("zhi")
    cos_all, sin_all = rope_tables()
    cos = lax.dynamic_index_in_dim(jnp.asarray(cos_all), zhi, 0, keepdims=False)
    sin = lax.dynamic_index_in_dim(jnp.asarray(sin_all), zhi, 0, keepdims=False)

    n_in, wq, ra, rb = run_first(normed, wq_blocks, wr_blocks)
    n_in, wq = n_in.reshape(1024, D), wq.reshape(D, QKV)
    qkv = dot_nn(n_in, wq).astype(BF)
    o, lse, q, kv, wg, wu, wd, wo, cotf = run_attend(qkv, cos, sin, w_out.astype(BF), ra, rb, cot)
    o_rows = o.reshape(1024, 256)
    wg, wu, wd = (w.reshape(D, SEG) for w in (wg, wu, wd))
    wo = wo.reshape(256, D)
    cotf = cotf.reshape(1024, D)
    part_o = dot_nn(o_rows, wo).astype(BF).reshape(8, 128, D)
    resid, n_mid = run_mid(part_o, tok)
    n_mid = n_mid.reshape(1024, D)
    gate, up = dot_nn(n_mid, wg), dot_nn(n_mid, wu)
    d_hidden = dot_nn(cotf, wd)
    sig = jax.nn.sigmoid(gate)
    silu = gate * sig
    hidden = (silu * up).astype(BF)
    d_gate = (d_hidden * up * sig * (1.0 + gate * (1.0 - sig))).astype(BF)
    d_up = (d_hidden * silu).astype(BF)
    part_m = (dot_nt(d_gate, wg) + dot_nt(d_up, wu)).astype(BF).reshape(8, 128, D)
    d_mid, d_attn = run_back(part_m, resid, cot)
    d_attn = d_attn.reshape(1024, D)
    part_b = dot_nt(hidden, wd).astype(BF).reshape(8, 128, D)
    gg, gu, gd = dot_tn(n_mid, d_gate), dot_tn(n_mid, d_up), dot_tn(cotf, hidden)
    gg, gu, gd = (g.astype(BF).reshape(4, 2, 4, 2, 2, 16, SEG) for g in (gg, gu, gd))
    d_o = dot_nt(d_attn, wo).astype(BF)
    go = dot_tn(o_rows, d_attn).astype(BF).reshape(4, 2, 2, 16, D)
    dqkv, block_out, fold, grad_out = run_attend_back(
        q, kv, lse, o, d_o.reshape(4, 256, 256), cos, sin, part_b, resid, gg, gu, gd, go
    )
    part_i = dot_nt(dqkv, wq).astype(BF).reshape(8, 128, D)
    gq = dot_tn(n_in, dqkv).astype(BF).reshape(4, 2, 4, 2, 2, 16, QKV)
    d_tokens, sum_q, sum_r = run_last(part_i, tok, d_mid, gq, fold)

    sum_q = sum_q.reshape(4, 2, 16, QKV).astype(F32)
    grad_q = sum_q[..., :256].reshape(4, 2, 16, 4, HEAD).transpose(2, 1, 3, 0, 4).reshape(16, D)
    grad_kv = jnp.sum(sum_q[..., 256:], axis=0).reshape(2, 16, 2, 2, HEAD)
    grad_kv = grad_kv.transpose(1, 3, 0, 2, 4).reshape(16, 512)
    raw_qkv = jnp.concatenate([grad_q, grad_kv], axis=1)
    sum_r = sum_r.astype(F32)
    raw_gu = sum_r[:, 0:2].transpose(2, 1, 0, 3).reshape(16, 2 * FF)
    grad_down = sum_r[:, 2].transpose(1, 0, 2).reshape(16, FF)
    grad_qkv = raw_qkv * gain[:, 0:1]
    grad_gu = raw_gu * gain[:, 1:2]
    grad_gains = jnp.stack(
        [jnp.sum(low_qkv * raw_qkv, axis=1), jnp.sum(low_gu * raw_gu, axis=1)], axis=1
    )

    first_q, second_q, weight_q = adam(w_qkv, grad_qkv, first_qkv, second_qkv, rate_matrix, decay_rate)
    first_o, second_o, weight_o = adam(w_out, grad_out, first_out, second_out, rate_matrix, decay_rate)
    first_g, second_g, weight_g = adam(
        w_gate_up, grad_gu, first_gate_up, second_gate_up, rate_matrix, decay_rate
    )
    first_d, second_d, weight_d = adam(
        w_down_t, grad_down, first_down, second_down, rate_matrix, decay_rate
    )
    first_n, second_n, weight_n = adam(gains, grad_gains, first_gains, second_gains, rate_gain, 0.0)
    return (
        block_out[None], d_tokens[None],
        first_q, second_q, weight_q, first_o, second_o, weight_o,
        first_g, second_g, weight_g, first_d, second_d, weight_d,
        first_n, second_n, weight_n,
    )


def solution(mesh):
    fine = Mesh(mesh.devices.reshape(4, 2, 4, 2, 2), ("x", "zlo", "y", "zhi", "core"))
    dp, seq = ("x", "zlo"), ("y", "zhi", "core")
    act, row = P(dp, seq, None), P(dp + seq, None)
    return jax.shard_map(
        local,
        mesh=fine,
        in_specs=(act, act) + (row,) * 15,
        out_specs=(act, act) + (row,) * 15,
        check_vma=False,
    )
```

time: 1950 us -> 508 us (0.26)
  waiting for transfers between devices: 1150 us -> 0 us
  Pallas kernels: 0 us -> 386 us
  blocking collectives: 179 us -> 0 us
  matrix products: 229 us -> 76.4 us
  local copies, waits for them, and re-layouts: 164 us -> 16.9 us
  other arithmetic: 123 us -> 17.1 us
  starting transfers between devices: 57.9 us -> 0 us
  loops' own time: 24 us -> 0 us
    all_gather x8 -> x0, waiting for transfers between devices: 1030 us -> none  [the longest x1 256 us: local(): lax.all_gather(low_shards[2], ('dp', 'seq'), axis=0, tiled=True)]
    pallas_call x0 -> x6, Pallas kernels: none -> 386 us  [the longest x1 96.9 us: run_attend(): pl.pallas_call(attend_kernel, out_shape=(shaped(4, 256, 256), shaped(4, 2...]
    all_gather x1 -> x0, blocking collectives: 179 us -> none  [local(): lax.all_gather(low_shards[4], ('dp', 'seq'), axis=0, tiled=True)]
    dot_general x40 -> x15, matrix products: 229 us -> 76.4 us  [the longest x5 30 us: dot_nn(): lax.dot_general(a, b, (((1,), (0,)), ((), ())), preferred_element_type=F32)]
    all_to_all x11 -> x0, waiting for transfers between devices: 74.1 us -> none  [the longest x1 11.8 us: local(): lax.all_to_all(owner_cols(acts_in, dp_parts, seq_parts).astype(jnp.bfloat...]
    all_to_all x11 -> x0, starting transfers between devices: 57.1 us -> none  [the longest x1 6.17 us: local(): lax.all_to_all(mixed_grad, 'seq', split_axis=1, concat_axis=0, tiled=True)]
    unnamed x143 -> x75, local copies, waits for them, and re-layouts: 55 us -> 1.76 us
    unnamed x10 -> x0, waiting for transfers between devices: 47.4 us -> none
  transfers between devices with their start and end apart: 20 -> 0, of which waited for: 19 -> 0; matrix products, arithmetic and copies ran while one was open for 12% -> 0% of each run, Pallas kernels for 0% -> 0%
where the time goes in v1:
time: 508 us; the launch traced here: 498 us
  Pallas kernels  386 us (76%)
  matrix products  76.4 us (15%)
  other arithmetic  17.1 us (3%)
  local copies, waits for them, and re-layouts  16.9 us (3%)
    pallas_call x1, Pallas kernels, run_attend(): pl.pallas_call(attend_kernel, out_shape=(shaped(4, 256, 256), shaped(4, 2...  96.9 us
    pallas_call x1, Pallas kernels, run_attend_back(): pl.pallas_call(attend_back_kernel, out_shape=(shaped(1024, QKV), shaped(1...  95 us
    pallas_call x1, Pallas kernels, run_first(): pl.pallas_call(first_kernel, out_shape=(shaped(8, 128, D), shaped(4, 2, 4...  52.7 us
    pallas_call x1, Pallas kernels, run_back(): pl.pallas_call(back_kernel, out_shape=(shaped(128, D, dtype=F32), shaped(...  51.8 us
    pallas_call x1, Pallas kernels, run_mid(): pl.pallas_call(mid_kernel, out_shape=(shaped(128, D, dtype=F32), shaped(8...  51.1 us
    pallas_call x1, Pallas kernels, run_last(): pl.pallas_call(last_kernel, out_shape=(shaped(128, D), shaped(8, 16, QKV)...  38.4 us
    dot_general x5, matrix products, dot_nn(): lax.dot_general(a, b, (((1,), (0,)), ((), ())), preferred_element_type=F32)  30 us
    dot_general x5, matrix products, dot_nt(): lax.dot_general(a, b, (((1,), (1,)), ((), ())), preferred_element_type=F32)  25.2 us

profile of v1, /device:TPU:1, one launch (start us, length us, event | category | flops | bytes accessed | tf_op | source)
XLA Modules:
  0.0 498.1 jit_solution(542532592177670156)
XLA Ops:
  0.7 1.3 fusion.1
  2.0 0.7 convert_convert_fusion
  2.7 1.5 convert_element_type.99.wout_ref
  4.2 1.0 fusion.7
  5.2 0.1 reshape.149
  5.3 0.1 reshape.150
  5.4 0.1 maximum_bitcast_fusion
  5.6 0.2 reshape.148
  5.7 0.1 copy.72
  5.8 0.1 concatenate.14
  6.0 0.7 pad_maximum_fusion.1.wq_ref
  6.6 1.0 convert_element_type.97
  7.6 0.0 copy-start.13
  7.6 0.2 reshape.153
  7.8 0.1 fusion.3
  8.0 0.2 reshape.151
  8.2 0.2 reshape.152
  8.4 0.1 copy_bitcast_fusion.1
  8.5 0.9 pad_maximum_fusion.wr_ref
  9.4 0.9 fusion.2.n_ref
  10.3 1.0 dynamic-slice_bitcast_fusion
  11.4 52.7 %first.1 = (bf16[8,128,2048]{2,1,0:T(8,128)(2,1)}, bf16[4,2,4,2,2,16,512]{6,5,4,3,2,1,0:T(8,128)(2,1)}, bf16[3,4,2,2,16,704]{5,4,3,2,1,0:T(8,128)(2,1)}, bf16[3,2,2,2,2,16,704]{6,5,4,3,2,1,0:T(8,128)(2,1)}) custom-call(bf16[128,2048]{1,0:T(8,128)(2,1)} %fusion.2.n_ref, bf16[8,16,512]{2,1,0:T(8,128)(2,1)} %pad_maximum_fusion.1.wq_ref, ...), custom_call_target="tpu_custom_call" | custom-call | tf_op jit(solution)/shard_map/first/pallas_call | solution.py:331
  64.1 6.2 %convolution_convert_fusion.8.qkv_ref = bf16[1024,512]{1,0:T(8,128)(2,1)} fusion(bf16[1024,2048]{1,0:T(8,128)(2,1)} %bitcast.131, bf16[2048,512]{1,0:T(8,128)(2,1)} %bitcast.147), kind=kOutput, calls=%fused_computation.14 | convolution fusion | flops 2148007936 | bytes 7340032 | tf_op jit(solution)/shard_map/dot_general | solution.py:358
  70.2 96.9 %attend.1 = (bf16[4,256,256]{2,1,0:T(8,128)(2,1)}, f32[4,2,1,512]{3,2,1,0:T(1,128)}, bf16[4,2,512,64]{3,2,1,0:T(8,128)(2,1)}, bf16[4,2,256,256]{3,2,1,0:T(8,128)...) custom-call(bf16[1024,512]{1,0:T(8,128)(2,1)} %convolution_convert_f, ...), custom_call_target="tpu_custom_call" | custom-call | tf_op jit(solution)/shard_map/attend/pallas_call | solution.py:561
  167.2 6.3 %fusion.19 = f32[1024,704]{0,1:T(8,128)S(1)} fusion(bf16[1024,2048]{1,0:T(8,128)(2,1)} %bitcast.133, bf16[2048,704]{1,0:T(8,128)(2,1)} %bitcast.145), kind=kOutput, calls=%fused_computation.71 | convolution fusion | flops 2952790016 | bytes 9961472 | tf_op jit(solution)/shard_map/dot_general | solution.py:358
  173.5 3.2 convolution_convert_fusion.2
  176.7 51.1 %mid.1 = (f32[128,2048]{1,0:T(8,128)}, bf16[8,128,2048]{2,1,0:T(8,128)(2,1)}) custom-call(bf16[8,128,2048]{2,1,0:T(8,128)(2,1)} %bitcast.104, bf16[128,2048]{1,0:T(8,128)(2,1)} %bitcast.108), custom_call_target="tpu_custom_call" | custom-call | tf_op jit(solution)/shard_map/mid/pallas_call | solution.py:613
  227.8 7.2 %fusion.20 = f32[1024,704]{0,1:T(8,128)} fusion(bf16[1024,2048]{1,0:T(8,128)(2,1)} %bitcast.135, bf16[2048,704]{1,0:T(8,128)(2,1)S(1)} %bitcast.144), kind=kOutput, calls=%fused_computation.72 | convolution fusion | flops 2952790016 | bytes 9961472 | tf_op jit(solution)/shard_map/dot_general | solution.py:358
  235.0 7.2 %multiply_convert_fusion = (bf16[1024,704]{0,1:T(8,128)(2,1)S(1)}, bf16[1024,704]{0,1:T(8,128)(2,1)}, bf16[1024,704]{0,1:T(8,128)(2,1)}) fusion(f32[1024,704]{0,1:T(8,128)} %fusion.20, f32[1024,704]{0,1:T(8,128)S(1)} %fusion.19, bf16[1024,2048]{1,0:T(8,128)(2,1)S(1)} %bitcast.137, bf16[2048,704]{1,0:T(8,128)(2,1)S(1)} %bitcast.141), kind=kOutput, calls=%fused_computation.8 | convolution fusion | flops 2963603456 | bytes 17170432 | tf_op jit(solution)/shard_map/dot_general | solution.py:358
  242.2 3.4 convolution_convert_fusion.3
  245.6 5.2 %convolution_convert_fusion.1 = bf16[1024,2048]{1,0:T(8,128)(2,1)} fusion(bf16[1024,704]{0,1:T(8,128)(2,1)S(1)} %get-tuple-element.80, bf16[2048,704]{1,0:T(8,128)(2,1)S(1)} %bitcast.146), kind=kOutput, calls=%fused_computation.2 | convolution fusion | flops 2954887168 | bytes 8519680 | tf_op jit(solution)/shard_map/dot_general | solution.py:350
  250.8 3.2 copy.60
  254.0 5.9 %convolution_convert_fusion.5 = bf16[2048,704]{0,1:T(8,128)(2,1)S(1)} fusion(bf16[1024,704]{0,1:T(8,128)(2,1)} %get-tuple-element.81, bf16[1024,2048]{1,0:T(8,128)(2,1)} %bitcast.136), kind=kOutput, calls=%fused_computation.6 | convolution fusion | flops 2954231808 | bytes 8519680 | tf_op jit(solution)/shard_map/dot_general | solution.py:354
  260.0 4.5 convolution_convert_fusion.4
  264.5 4.7 copy.59
  269.2 2.8 copy.58
  272.0 6.0 %fusion.21 = f32[1024,2048]{1,0:T(8,128)S(1)} fusion(bf16[1024,704]{0,1:T(8,128)(2,1)} %get-tuple-element.81, bf16[2048,704]{1,0:T(8,128)(2,1)} %bitcast.143), kind=kOutput, calls=%fused_computation.73 | convolution fusion | flops 2952790016 | bytes 12713984 | tf_op jit(solution)/shard_map/dot_general | solution.py:350
  278.0 5.2 %add_convert_fusion = bf16[1024,2048]{1,0:T(8,128)(2,1)} fusion(f32[1024,2048]{1,0:T(8,128)S(1)} %fusion.21, bf16[1024,704]{0,1:T(8,128)(2,1)S(1)} %copy-done.35, bf16[2048,704]{1,0:T(8,128)(2,1)S(1)} %bitcast.142), kind=kOutput, calls=%fused_computation | convolution fusion | flops 2956984320 | bytes 16908288 | tf_op jit(solution)/shard_map/dot_general | solution.py:350
  283.2 51.8 %back.1 = (f32[128,2048]{1,0:T(8,128)}, bf16[8,128,2048]{2,1,0:T(8,128)(2,1)}) custom-call(bf16[8,128,2048]{2,1,0:T(8,128)(2,1)} %bitcast.111, f32[128,2048]{1,0:T(8,128)} %get-tuple-element.55.resid_ref, bf16[128,2048]{1,0:T(8,128)(2,1)} %bitcast.117), custom_call_target="tpu_custom_call" | custom-call | tf_op jit(solution)/shard_map/back/pallas_call | solution.py:661
  335.0 4.4 convolution_convert_fusion.9
  339.5 2.3 convolution_convert_fusion.7
  341.7 95.0 %attend_back.1 = (bf16[1024,512]{1,0:T(8,128)(2,1)}, bf16[128,2048]{1,0:T(8,128)(2,1)}, bf16[3,4,2,16,704]{4,3,2,1,0:T(8,128)(2,1)}, f32[16,2048]{1,0:T(8,128)}) custom-call(bf16[4,2,512,64]{3,2,1,0:T(8,128)(2,1)} %get-tuple-element.45.q_ref, bf16[4,2,256,256]{3,2,1,0:T(8,128)(2,1)} %get-tuple-element.46.kv_ref, f32[4,2,1,512]{3,2,1,0:T(1,128)} %get-tuple-element.47.lse_ref, ...), custom_call_target="tpu_custom_call" | custom-call | tf_op jit(solution)/shard_map/attend_back/pallas_call | solution.py:959
  436.8 5.1 %convolution_convert_fusion.6 = bf16[2048,512]{1,0:T(8,128)(2,1)} fusion(bf16[1024,2048]{1,0:T(8,128)(2,1)S(1)} %bitcast.132, bf16[1024,512]{1,0:T(8,128)(2,1)} %get-tuple-element.58), kind=kOutput, calls=%fused_computation.7 | convolution fusion | flops 2148532224 | bytes 7340032 | tf_op jit(solution)/shard_map/dot_general | solution.py:354
  441.9 0.8 multiply_subtract_fusion.3
  442.7 4.4 convolution_convert_fusion
  447.1 38.4 %last.1 = (bf16[128,2048]{1,0:T(8,128)(2,1)}, bf16[8,16,512]{2,1,0:T(8,128)(2,1)}, bf16[8,3,16,704]{3,2,1,0:T(8,128)(2,1)}) custom-call(bf16[8,128,2048]{2,1,0:T(8,128)(2,1)} %bitcast.110, bf16[128,2048]{1,0:T(8,128)(2,1)} %bitcast.109, f32[128,2048]{1,0:T(8,128)} %get-tuple-element.59.dmid_ref, bf16[4,2,4,2,2,16,512]{6,5,4,3,2,1,0:T(8,128)(2,1)} %bitcast.115, ...), custom_call_target="tpu_custom_call" | custom-call | tf_op jit(solution)/shard_map/last/pallas_call | solution.py:1029
  485.5 1.0 bitcast_convert_fusion
  486.6 0.1 reshape.176
  486.7 0.1 reshape.177
  486.8 0.2 reshape.174
  487.0 0.2 copy.70
  487.2 0.2 reshape.175
  487.5 1.0 multiply_subtract_fusion.2
  488.5 0.1 convert_element_type.115
  488.7 0.1 slice_bitcast_fusion
  488.7 0.5 copy.63
  489.2 0.3 reshape.178
  489.6 0.2 copy.64
  489.8 0.1 reshape.179
  490.0 2.2 multiply_subtract_fusion.1
  492.3 3.1 multiply_subtract_fusion
  495.4 0.6 multiply_subtract_fusion.4
  496.0 0.8 copy.76
  496.8 0.8 copy.77
  (85 shorter events, 0.4 us)
Async XLA Ops:
  0.7 7.2 %copy-start.2 = (f32[16,11264]{1,0:T(8,128)S(1)}, f32[16,11264]{1,0:T(8,128)}, u32[]{:S(2)}) copy-start(f32[16,11264]{1,0:T(8,128)} %param.23) | copy-start | bytes 2162692
  5.8 3.6 copy-start
  7.6 2.7 copy-start.13
  8.4 1.9 copy-start.14
  167.2 6.3 %copy-start.1 = (bf16[4,256,256]{2,1,0:T(8,128)(2,1)S(1)}, bf16[4,256,256]{2,1,0:T(8,128)(2,1)}, u32[]{:S(2)}) copy-start(bf16[4,256,256]{2,1,0:T(8,128)(2,1)} %get-tuple-element.48.o_ref) | copy-start | bytes 1572868
  167.2 6.3 %copy-start.5 = (bf16[4,2,2,16,2048]{4,3,2,1,0:T(8,128)(2,1)S(1)}, bf16[4,2,2,16,2048]{4,3,2,1,0:T(8,128)(2,1)}, u32[]{:S(2)}) copy-start(bf16[4,2,2,16,2048]{4,3,2,1,0:T(8,128)(2,1)} %get-tuple-element.51) | copy-start | bytes 3145732
  176.7 51.1 %copy-start.30 = (bf16[4,2,4,2,2,16,704]{6,5,4,3,2,1,0:T(8,128)(2,1)S(1)}, bf16[4,2,4,2,2,16,704]{6,5,4,3,2,1,0:T(8,128)(2,1)}, u32[]{:S(2)}) copy-start(bf16[4,2,4,2,2,16,704]{6,5,4,3,2,1,0:T(8,128)(2,1)} %get-tuple-element.54) | copy-start | bytes 8650756
  227.8 7.2 %copy-start.25 = (bf16[8,128,2048]{2,1,0:T(8,128)(2,1)S(1)}, bf16[8,128,2048]{2,1,0:T(8,128)(2,1)}, u32[]{:S(2)}) copy-start(bf16[8,128,2048]{2,1,0:T(8,128)(2,1)} %get-tuple-element.52) | copy-start | bytes 12582916
  227.8 7.2 %copy-start.28 = (bf16[4,2,4,2,2,16,704]{6,5,4,3,2,1,0:T(8,128)(2,1)S(1)}, bf16[4,2,4,2,2,16,704]{6,5,4,3,2,1,0:T(8,128)(2,1)}, u32[]{:S(2)}) copy-start(bf16[4,2,4,2,2,16,704]{6,5,4,3,2,1,0:T(8,128)(2,1)} %get-tuple-element.53) | copy-start | bytes 8650756
  235.0 7.2 %copy-start.24 = (bf16[8,128,2048]{2,1,0:T(8,128)(2,1)S(1)}, bf16[8,128,2048]{2,1,0:T(8,128)(2,1)}, u32[]{:S(2)}) copy-start(bf16[8,128,2048]{2,1,0:T(8,128)(2,1)} %get-tuple-element.49) | copy-start | bytes 12582916
  242.2 3.4 copy-start.31
  254.0 5.9 %copy-start.26 = (bf16[8,128,2048]{2,1,0:T(8,128)(2,1)S(1)}, bf16[8,128,2048]{2,1,0:T(8,128)(2,1)}, u32[]{:S(2)}) copy-start(bf16[8,128,2048]{2,1,0:T(8,128)(2,1)} %get-tuple-element.52) | copy-start | bytes 12582916
  254.0 5.9 %copy-start.34 = (bf16[1024,704]{0,1:T(8,128)(2,1)S(1)}, bf16[1024,704]{0,1:T(8,128)(2,1)}, u32[]{:S(2)}) copy-start(bf16[1024,704]{0,1:T(8,128)(2,1)} %get-tuple-element.82) | copy-start | bytes 4325380
  272.0 6.0 %copy-start.29 = (bf16[4,2,4,2,2,16,704]{6,5,4,3,2,1,0:T(8,128)(2,1)S(1)}, bf16[4,2,4,2,2,16,704]{6,5,4,3,2,1,0:T(8,128)(2,1)}, u32[]{:S(2)}) copy-start(bf16[4,2,4,2,2,16,704]{6,5,4,3,2,1,0:T(8,128)(2,1)} %get-tuple-element.53) | copy-start | bytes 8650756
  272.0 6.0 %copy-start.35 = (bf16[1024,704]{0,1:T(8,128)(2,1)S(1)}, bf16[1024,704]{0,1:T(8,128)(2,1)}, u32[]{:S(2)}) copy-start(bf16[1024,704]{0,1:T(8,128)(2,1)} %get-tuple-element.82) | copy-start | bytes 4325380
  283.2 51.8 %copy-start.6 = (bf16[4,2,2,16,2048]{4,3,2,1,0:T(8,128)(2,1)S(1)}, bf16[4,2,2,16,2048]{4,3,2,1,0:T(8,128)(2,1)}, u32[]{:S(2)}) copy-start(bf16[4,2,2,16,2048]{4,3,2,1,0:T(8,128)(2,1)} %get-tuple-element.51) | copy-start | bytes 3145732
  335.0 4.4 copy-start.27
  341.7 95.0 %copy-start.23 = (bf16[8,128,2048]{2,1,0:T(8,128)(2,1)S(1)}, bf16[8,128,2048]{2,1,0:T(8,128)(2,1)}, u32[]{:S(2)}) copy-start(bf16[8,128,2048]{2,1,0:T(8,128)(2,1)} %get-tuple-element.41) | copy-start | bytes 12582916
  436.7 5.2 %copy-start.10 = (f32[16,2048]{1,0:T(8,128)S(1)}, f32[16,2048]{1,0:T(8,128)}, u32[]{:S(2)}) copy-start(f32[16,2048]{1,0:T(8,128)} %param.22) | copy-start | bytes 393220
  436.7 5.1 %copy-start.17 = (f32[16,2048]{1,0:T(8,128)S(1)}, f32[16,2048]{1,0:T(8,128)}, u32[]{:S(2)}) copy-start(f32[16,2048]{1,0:T(8,128)} %param.29) | copy-start | bytes 393220
  436.8 5.1 %copy-start.18 = (f32[16,2048]{1,0:T(8,128)S(1)}, f32[16,2048]{1,0:T(8,128)}, u32[]{:S(2)}) copy-start(f32[16,2048]{1,0:T(8,128)} %param.28) | copy-start | bytes 393220
  436.8 5.1 %copy-start.19 = (f32[16,2048]{1,0:T(8,128)S(1)}, f32[16,2048]{1,0:T(8,128)}, u32[]{:S(2)}) copy-start(f32[16,2048]{1,0:T(8,128)} %get-tuple-element.63) | copy-start | bytes 393220
  436.8 5.9 %copy-start.32 = (bf16[4,2,4,2,2,16,512]{6,5,4,3,2,1,0:T(8,128)(2,1)S(1)}, bf16[4,2,4,2,2,16,512]{6,5,4,3,2,1,0:T(8,128)(2,1)}, u32[]{:S(2)}) copy-start(bf16[4,2,4,2,2,16,512]{6,5,4,3,2,1,0:T(8,128)(2,1)} %get-tuple-element.42) | copy-start | bytes 6291460
  436.8 5.9 %copy-start.33 = (bf16[1024,512]{1,0:T(8,128)(2,1)S(1)}, bf16[1024,512]{1,0:T(8,128)(2,1)}, u32[]{:S(2)}) copy-start(bf16[1024,512]{1,0:T(8,128)(2,1)} %get-tuple-element.58) | copy-start | bytes 3145732
  447.1 40.3 %copy-start.8 = (f32[16,2560]{1,0:T(8,128)S(1)}, f32[16,2560]{1,0:T(8,128)}, u32[]{:S(2)}) copy-start(f32[16,2560]{1,0:T(8,128)} %param.21) | copy-start | bytes 491524
  447.1 40.3 %copy-start.15 = (f32[16,2560]{1,0:T(8,128)S(1)}, f32[16,2560]{1,0:T(8,128)}, u32[]{:S(2)}) copy-start(f32[16,2560]{1,0:T(8,128)} %param.27) | copy-start | bytes 491524
  447.1 40.3 %copy-start.16 = (f32[16,2560]{1,0:T(8,128)S(1)}, f32[16,2560]{1,0:T(8,128)}, u32[]{:S(2)}) copy-start(f32[16,2560]{1,0:T(8,128)} %param.26) | copy-start | bytes 491524
  485.5 3.0 copy-start.9
  488.7 1.3 copy-start.4
  489.2 3.0 copy-start.3
  489.6 2.7 copy-start.7
  492.2 3.2 copy-start.20
  492.2 3.2 copy-start.21
  492.2 3.2 copy-start.22
  492.2 3.8 copy-start.11
  492.2 4.6 copy-start.12
